TPU v7x, 768 devices: a whole 4x8x12 slice. The times are simulated.
768 devices in a mesh: lat: 16 (over y_hi, x), lon: 48 (over z, y_lo, core).
Axes of the slice: x: 4, y: 8 (y_hi: 4, y_lo: 2; y = y_hi * 2 + y_lo), z: 12, core: 2. Of those that a mesh axis runs over, the one named last changes fastest.
Arguments:
- swath_input: bfloat16 [1536, 64, 64, 256], P(('lat', 'lon')), may hold values from -6 to 6
- conv_weight: bfloat16 [3, 3, 256, 256], replicated, may hold values from -0.125 to 0.125
- conv_bias: float32 [256], replicated, may hold values from -3 to 3
- block_band: int32 [1536, 1], P(('lat', 'lon')), may hold values from 0 to 15, as said below
- row_offset: int32 [1536], P(('lat', 'lon')), may hold values from 0 to 8
- col_offset: int32 [1536], P(('lat', 'lon')), may hold values from 0 to 8
- row_weights: bfloat16 [1536, 16, 32], P(('lat', 'lon')), may hold values from -1 to 1
- col_weights: bfloat16 [1536, 16, 32], P(('lat', 'lon')), may hold values from -1 to 1
- background: bfloat16 [384, 1152, 256], P('lat', 'lon'), may hold values from -6 to 6
- depth_weight: float32 [2, 7, 7, 256], replicated, may hold values from -0.875 to 0.875
- norm_gain: float32 [2, 256], replicated, may hold values from 0.1 to 1.9
- up_weight: bfloat16 [2, 256, 1024], replicated, may hold values from -0.375 to 0.375
- down_weight: bfloat16 [2, 1024, 256], replicated, may hold values from -0.1875 to 0.1875
Outputs:
- weather_grid: bfloat16 [384, 1152, 256], P('lat', 'lon')
Inputs may be any that keep to these rules, and one draw needn't show every extreme that they name: `block_band`: block b's band is the latitude band (b // 2) // 48 of the device that holds it, or one next to it; every device sends at least one block to a neighbouring band, at most 2 to each, and some device sends exactly 2 to one.
All inputs are finite; a program needn't handle non-finite values.
Results may differ from a plain program's by a relative error of at most 0.011.
Values may be sent and summed in bfloat16 or wider, within the bound.
A program may use at most 64 MiB of HBM per device.

v0:
```python
import jax
import jax.numpy as jnp
from jax import lax
from jax.sharding import PartitionSpec as P

KS = 7
HALO = 3
LAYERS = 2
CAP = 2
RB = 16
RW = 16


def shifted(value, axis, steps):
    count = lax.axis_size(axis)
    leading, last = (max(0, -steps), min(count, count - steps))
    return lax.ppermute(value, axis, [(source, source + steps) for source in range(leading, last)])


def with_halo(value, sides, width, wrap):
    for axis, dim in sides:
        size, length = (lax.axis_size(axis), value.shape[dim])
        up = [(i, (i + 1) % size) for i in range(size if wrap else size - 1)]
        down = [(j, i) for i, j in up]
        last = lax.slice_in_dim(value, length - width, length, axis=dim)
        leading = lax.slice_in_dim(value, 0, width, axis=dim)
        before = lax.ppermute(last, axis, up)
        after = lax.ppermute(leading, axis, down)
        value = jnp.concatenate([before, value, after], axis=dim)
    return value


def resample_local(blocks, row_mix, col_mix):
    row_mixed = jnp.einsum("nri,nijc->nrjc", row_mix, blocks, preferred_element_type=jnp.float32)
    both_mixed = jnp.einsum(
        "nrjc,nuj->nruc", row_mixed, col_mix.astype(jnp.float32), precision=lax.Precision.HIGHEST
    )
    return both_mixed.astype(jnp.bfloat16)


def place_rows(onehot, values):
    flat_values = values.reshape(values.shape[0], -1)
    placed = jnp.dot(onehot.astype(values.dtype), flat_values, preferred_element_type=jnp.float32)
    return placed.astype(values.dtype).reshape((onehot.shape[0],) + values.shape[1:])


def place_ints(onehot, values):
    return jnp.sum(jnp.where(onehot, values[None, :], 0), axis=1)


def keep_local(keep, values):
    shaped = keep.reshape((keep.shape[0],) + (1,) * (values.ndim - 1))
    return jnp.where(shaped, values, jnp.zeros_like(values))


def layer_apply(padded, depth_kernel, gain, up_matrix, down_matrix):
    height = padded.shape[0] - (KS - 1)
    width = padded.shape[1] - (KS - 1)
    channels = padded.shape[2]
    widened = padded.astype(jnp.float32)
    kernel = depth_kernel.reshape(KS, KS, 1, channels)
    mixed = lax.conv_general_dilated(
        widened[None],
        kernel,
        (1, 1),
        ((0, 0), (0, 0)),
        dimension_numbers=("NHWC", "HWIO", "NHWC"),
        feature_group_count=channels,
        precision=lax.Precision.HIGHEST,
    )[0]
    centered = mixed - jnp.mean(mixed, axis=-1, keepdims=True)
    variance = jnp.mean(centered * centered, axis=-1, keepdims=True)
    normed = (centered * lax.rsqrt(variance + 1e-06) * gain).astype(jnp.bfloat16)
    flat_cells = normed.reshape(height * width, -1)
    hidden = jax.nn.gelu(jnp.dot(flat_cells, up_matrix, preferred_element_type=jnp.float32)).astype(
        jnp.bfloat16
    )
    output = jnp.dot(hidden, down_matrix, preferred_element_type=jnp.float32).reshape(
        height, width, -1
    )
    residual_part = widened[HALO : HALO + height, HALO : HALO + width]
    return (residual_part + output).astype(jnp.bfloat16)


def per_device(
    swath_input,
    conv_weight,
    conv_bias,
    block_band,
    row_offset,
    col_offset,
    row_weights,
    col_weights,
    background,
    depth_weight,
    norm_gain,
    up_weight,
    down_weight,
):
    blocks_here = swath_input.shape[0]
    tile_rows = background.shape[0]
    tile_cols = background.shape[1]
    convolved = lax.conv_general_dilated(
        swath_input,
        conv_weight,
        (2, 2),
        ((1, 1), (1, 1)),
        dimension_numbers=("NHWC", "HWIO", "NHWC"),
        preferred_element_type=jnp.float32,
    )
    features = jax.nn.gelu(convolved + conv_bias).astype(jnp.bfloat16)
    own_band = lax.axis_index("lat")
    offset_band = block_band[:, 0] - own_band
    staying = offset_band == 0
    positions = jnp.arange(blocks_here, dtype=jnp.int32)
    row_list = [row_offset]
    col_list = [col_offset]
    block_list = [keep_local(staying, features)]
    rowmix_list = [row_weights]
    colmix_list = [col_weights]
    for step in (1, -1):
        going = offset_band == step
        earlier = jnp.sum(going[None, :] & (positions[None, :] < positions[:, None]), axis=1)
        table = (jnp.arange(CAP, dtype=jnp.int32)[:, None] == earlier[None, :]) & going[None, :]
        got_blocks, got_rowmix, got_colmix, got_rows, got_cols = shifted(
            (
                place_rows(table, features),
                place_rows(table, row_weights),
                place_rows(table, col_weights),
                place_ints(table, row_offset),
                place_ints(table, col_offset),
            ),
            "lat",
            step,
        )
        block_list.append(got_blocks)
        rowmix_list.append(got_rowmix)
        colmix_list.append(got_colmix)
        row_list.append(got_rows)
        col_list.append(got_cols)
    arrived = resample_local(
        jnp.concatenate(block_list, axis=0),
        jnp.concatenate(rowmix_list, axis=0),
        jnp.concatenate(colmix_list, axis=0),
    )
    all_rows = jnp.concatenate(row_list, axis=0)
    all_cols = jnp.concatenate(col_list, axis=0)
    row_place = (
        jnp.arange(tile_rows, dtype=jnp.int32)[None, :, None]
        == all_rows[:, None, None] + jnp.arange(RB, dtype=jnp.int32)[None, None, :]
    ).astype(jnp.bfloat16)
    col_place = (
        jnp.arange(tile_cols, dtype=jnp.int32)[None, :, None]
        == all_cols[:, None, None] + jnp.arange(RW, dtype=jnp.int32)[None, None, :]
    ).astype(jnp.bfloat16)
    lifted = jnp.einsum(
        "shr,sruc->shuc", row_place, arrived, preferred_element_type=jnp.float32
    ).astype(jnp.bfloat16)
    summed = jnp.einsum("swu,shuc->hwc", col_place, lifted, preferred_element_type=jnp.float32)
    state = (background.astype(jnp.float32) + summed).astype(jnp.bfloat16)
    for layer_index in range(LAYERS):
        widened = with_halo(state, (("lon", 1),), HALO, True)
        widened = with_halo(widened, (("lat", 0),), HALO, False)
        state = layer_apply(
            widened,
            depth_weight[layer_index],
            norm_gain[layer_index],
            up_weight[layer_index],
            down_weight[layer_index],
        )
    return state


def solution(mesh):
    in_specs = (
        P(("lat", "lon"), None, None, None),
        P(),
        P(),
        P(("lat", "lon"), None),
        P(("lat", "lon")),
        P(("lat", "lon")),
        P(("lat", "lon"), None, None),
        P(("lat", "lon"), None, None),
        P("lat", "lon", None),
        P(),
        P(),
        P(),
        P(),
    )
    out_specs = P("lat", "lon", None)
    return jax.shard_map(
        per_device, mesh=mesh, in_specs=in_specs, out_specs=out_specs, check_vma=False
    )
```

profile of v0, /device:TPU:22, one launch (start us, length us, event | category | flops | bytes accessed | tf_op | source)
XLA Modules:
  0.0 191.8 jit_solution(6660548429161395106)
XLA Ops:
  0.0 4.7 %copy.82 = bf16[2,64,64,256]{3,1,2,0:T(8,128)(2,1)S(1)} copy(bf16[2,64,64,256]{3,2,1,0:T(8,128)(2,1)} %param.13) | data formatting | bytes 8388608 | tf_op args[0]
  5.5 3.3 %fusion.1 = bf16[64,2,8,12,256]{4,0,3,2,1:T(8,128)(2,1)S(1)} fusion(bf16[64,2,7,2,256]{4,0,3,2,1:T(8,128)(2,1)S(1)} %slice.79, bf16[64,2,8,10,256]{4,0,3,2,1:T(8,128)(2,1)S(1)} %bitcast.126), kind=kLoop, calls=%fused_computation.4 | loop fusion | flops 18874368 | bytes 12451840 | tf_op jit(solution)/shard_map/conv_general_dilated | solution.py:103
  9.1 7.1 %copy_select_fusion = (bf16[32,16,5,256]{3,1,2,0:T(8,128)(2,1)}, bf16[32,16,5,256]{3,1,2,0:T(8,128)(2,1)S(1)}) fusion(pred[32,16,5,256]{3,0,2,1:T(32,128)(4,1)S(1)} %bitcast.137, f32[256]{0:T(256)S(1)} %copy-done.11, bf16[3,3,256,256]{3,2,1,0:T(8,128)(2,1)S(1)} %copy-done, bf16[64,2,8,12,256]{4,0,3,2,1:T(8,128)(2,1)S(1)} %fusion.1, ...), kind=kOutput, calls=%fused_computation.28 | convolution fusion | flops 2996305920 | bytes 10749008 | tf_op jit(solution)/shard_map/conv_general_dilated | solution.py:103
  17.3 1.1 copy.49
  19.3 1.2 convolution_convert_fusion.1
  21.3 5.8 %collective-permute-start.6 = (bf16[2,32,32,256]{3,1,2,0:T(8,128)(2,1)S(1)}, bf16[2,32,32,256]{3,1,2,0:T(8,128)(2,1)}, u32[]{:S(2)}, u32[]{:S(2)}) collective-permute-start(bf16[2,32,32,256]{3,1,2,0:T(8,128)(2,1)S(1)} %copy.34), channel_id=1, source_target_pairs={{0,48},{48,96},{96,144},{144,192},{192,240},{240,288},{288,336},{3... | collective-permute-start | bytes 3145736 | tf_op jit(solution)/shard_map/ppermute | solution.py:17
  27.1 1.2 convolution_convert_fusion
  28.6 1.5 copy.35
  30.1 1.9 collective-permute-start.7
  32.9 8.1 %collective-permute-start.4 = (bf16[2,16,32]{2,1,0:T(8,128)(2,1)}, bf16[2,16,32]{2,1,0:T(8,128)(2,1)}, u32[]{:S(2)}, u32[]{:S(2)}) collective-permute-start(bf16[2,16,32]{2,1,0:T(8,128)(2,1)} %reshape.188), channel_id=1, source_target_pairs={{0,48},{48,96},{96,144},{144,192},{192,240},{240,288},{288,336},{3... | collective-permute-start | bytes 6152 | tf_op jit(solution)/shard_map/ppermute | solution.py:17
  41.9 1.9 collective-permute-start.5
  43.8 8.1 %collective-permute-start = (s32[2]{0:T(128)}, s32[2]{0:T(128)}, u32[]{:S(2)}, u32[]{:S(2)}) collective-permute-start(s32[2]{0:T(128)} %get-tuple-element.8), channel_id=1, source_target_pairs={{0,48},{48,96},{96,144},{144,192},{192,240},{240,288},{288,336},{3... | collective-permute-start | bytes 32 | tf_op jit(solution)/shard_map/ppermute | solution.py:17
  53.4 1.7 copy.31
  55.2 1.3 reshape.185
  56.5 1.3 reshape.186
  57.9 14.2 %collective-permute-done = s32[2]{0:T(128)} collective-permute-done((s32[2]{0:T(128)}, s32[2]{0:T(128)}, u32[]{:S(2)}, u32[]{:S(2)}) %collective-permute-start) | collective-permute-done | bytes 40 | tf_op jit(solution)/shard_map/ppermute | solution.py:17
  72.1 1.9 collective-permute-start.1
  74.1 9.1 %collective-permute-done.1 = s32[2]{0:T(128)S(1)} collective-permute-done((s32[2]{0:T(128)}, s32[2]{0:T(128)S(1)}, u32[]{:S(2)}, u32[]{:S(2)}) %collective-permute-start.1) | collective-permute-done | bytes 40 | tf_op jit(solution)/shard_map/ppermute | solution.py:17
  83.2 3.2 %collective-permute-start.8 = (s32[2]{0:T(128)}, s32[2]{0:T(128)S(1)}, u32[]{:S(2)}, u32[]{:S(2)}) collective-permute-start(s32[2]{0:T(128)} %get-tuple-element.5), channel_id=1, source_target_pairs={{0,48},{48,96},{96,144},{144,192},{192,240},{240,288},{288,336},{3... | collective-permute-start | bytes 32 | tf_op jit(solution)/shard_map/ppermute | solution.py:17
  86.4 0.7 pad_add_fusion
  87.1 1.5 collective-permute-done.8
  88.6 1.9 collective-permute-start.9
  90.6 7.9 %collective-permute-done.9 = s32[2]{0:T(128)S(1)} collective-permute-done((s32[2]{0:T(128)}, s32[2]{0:T(128)S(1)}, u32[]{:S(2)}, u32[]{:S(2)}) %collective-permute-start.9) | collective-permute-done | bytes 40 | tf_op jit(solution)/shard_map/ppermute | solution.py:17
  98.5 3.2 %collective-permute-start.2 = (bf16[2,16,32]{2,1,0:T(8,128)(2,1)}, bf16[2,16,32]{2,1,0:T(8,128)(2,1)S(1)}, u32[]{:S(2)}, u32[]{:S(2)}) collective-permute-start(bf16[2,16,32]{2,1,0:T(8,128)(2,1)} %reshape.185), channel_id=1, source_target_pairs={{0,48},{48,96},{96,144},{144,192},{192,240},{240,288},{288,336},{3... | collective-permute-start | bytes 6152 | tf_op jit(solution)/shard_map/ppermute | solution.py:17
  102.6 2.6 %collective-permute-start.3 = (bf16[2,16,32]{2,1,0:T(8,128)(2,1)}, bf16[2,16,32]{2,1,0:T(8,128)(2,1)S(1)}, u32[]{:S(2)}, u32[]{:S(2)}) collective-permute-start(bf16[2,16,32]{2,1,0:T(8,128)(2,1)} %reshape.186), channel_id=1, source_target_pairs={{48,0},{96,48},{144,96},{192,144},{240,192},{288,240},{336,288},{3... | collective-permute-start | bytes 6152 | tf_op jit(solution)/shard_map/ppermute | solution.py:17
  105.2 2.1 %fusion.5 = f32[6,16,32,256]{3,1,2,0:T(8,128)S(1)} fusion(bf16[2,32,32,256]{3,1,2,0:T(8,128)(2,1)} %collective-permute-done.7, bf16[2,32,32,256]{3,1,2,0:T(8,128)(2,1)} %collective-permute-done.6, bf16[2,32,32,256]{3,1,2,0:T(8,128)(2,1)S(1)} %slice_bitcast_fusion.1, bf16[2,16,32]{2,1,0:T(8,128)(2,1)} %collective-permute-done.5, ...), kind=kOutput, calls=%fused_computation.12 | convolution fusion | flops 59787264 | bytes 6297600 | tf_op jit(solution)/shard_map/nri,nijc->nrjc/dot_general | solution.py:34
  107.4 5.1 %collective-permute-done.3 = bf16[2,16,32]{2,1,0:T(8,128)(2,1)S(1)} collective-permute-done((bf16[2,16,32]{2,1,0:T(8,128)(2,1)}, bf16[2,16,32]{2,1,0:T(8,128)(2,1)S(1)}, u32[]{:S(2)}, u32[]{:S(2)}) %collective-permute-start.3) | collective-permute-done | bytes 2080 | tf_op jit(solution)/shard_map/ppermute | solution.py:17
  112.5 3.0 %fusion.42 = bf16[6,16,16,256]{3,2,1,0:T(8,128)(2,1)S(1)} fusion(f32[6,16,32,256]{3,1,2,0:T(8,128)S(1)} %fusion.5, bf16[2,16,32]{2,1,0:T(8,128)(2,1)S(1)} %collective-permute-done.3, bf16[2,16,32]{2,1,0:T(8,128)(2,1)S(1)} %collective-permute-done.2, bf16[2,16,32]{2,1,0:T(8,128)(2,1)S(1)} %copy-done.2), kind=kOutput, calls=%fused_computation.47 | convolution fusion | flops 151406592 | bytes 3938304 | tf_op jit(solution)/shard_map/nrjc,nuj->nruc/dot_general | solution.py:35
  115.6 0.8 convolution_convert_fusion.2
  116.9 1.9 %collective-permute-start.10 = (bf16[24,3,256]{2,1,0:T(4,128)(2,1)S(1)}, bf16[24,3,256]{2,1,0:T(4,128)(2,1)S(1)}, u32[]{:S(2)}, u32[]{:S(2)}) collective-permute-start(bf16[24,3,256]{2,1,0:T(4,128)(2,1)S(1)} %get-tuple-element.17), channel_id=1, source_target_pairs={{0,1},{1,2},{2,3},{3,4},{4,5},{5,6},{6,7},{7,8},{8,9},{9,10},{10,1... | collective-permute-start | bytes 110600 | tf_op jit(solution)/shard_map/ppermute | solution.py:27
  118.8 9.6 %collective-permute-start.11 = (bf16[24,3,256]{2,1,0:T(4,128)(2,1)S(1)}, bf16[24,3,256]{2,1,0:T(4,128)(2,1)S(1)}, u32[]{:S(2)}, u32[]{:S(2)}) collective-permute-start(bf16[24,3,256]{2,1,0:T(4,128)(2,1)S(1)} %get-tuple-element.18), channel_id=1, source_target_pairs={{1,0},{2,1},{3,2},{4,3},{5,4},{6,5},{7,6},{8,7},{9,8},{10,9},{11,1... | collective-permute-start | bytes 110600 | tf_op jit(solution)/shard_map/ppermute | solution.py:28
  128.4 1.7 collective-permute-done.11
  130.1 3.2 %collective-permute-start.12 = (bf16[3,30,256]{2,1,0:T(8,128)(2,1)S(1)}, bf16[3,30,256]{2,1,0:T(8,128)(2,1)S(1)}, u32[]{:S(2)}, u32[]{:S(2)}) collective-permute-start(bf16[3,30,256]{2,1,0:T(8,128)(2,1)S(1)} %get-tuple-element.13), channel_id=1, source_target_pairs={{0,48},{48,96},{96,144},{144,192},{192,240},{240,288},{288,336},{3... | collective-permute-start | bytes 138248 | tf_op jit(solution)/shard_map/ppermute | solution.py:27
  133.3 2.9 %collective-permute-start.13 = (bf16[3,30,256]{2,1,0:T(8,128)(2,1)S(1)}, bf16[3,30,256]{2,1,0:T(8,128)(2,1)S(1)}, u32[]{:S(2)}, u32[]{:S(2)}) collective-permute-start(bf16[3,30,256]{2,1,0:T(8,128)(2,1)S(1)} %get-tuple-element.14), channel_id=1, source_target_pairs={{48,0},{96,48},{144,96},{192,144},{240,192},{288,240},{336,288},{3... | collective-permute-start | bytes 138248 | tf_op jit(solution)/shard_map/ppermute | solution.py:28
  136.3 7.2 %collective-permute-done.13 = bf16[3,30,256]{2,1,0:T(8,128)(2,1)S(1)} collective-permute-done((bf16[3,30,256]{2,1,0:T(8,128)(2,1)S(1)}, bf16[3,30,256]{2,1,0:T(8,128)(2,1)S(1)}, u32[]{:S(2)}, u32[]{:S(2)}) %collective-permute-start.13) | collective-permute-done | bytes 46112 | tf_op jit(solution)/shard_map/ppermute | solution.py:28
  143.7 9.3 %fusion.92 = (f32[24,24]{1,0:T(8,128)S(1)}, f32[1,24,24,256]{3,0,2,1:T(1,128)S(1)}) fusion(f32[2,7,7,256]{3,0,2,1:T(2,128)S(1)} %copy-done.10, bf16[1,30,30,256]{3,2,1,0:T(8,128)(2,1)S(1)} %maximum_bitcast_fusion), kind=kOutput, calls=%fused_computation.139 | convolution fusion | flops 86851008 | bytes 1133824 | tf_op jit(solution)/shard_map/conv_general_dilated | solution.py:62
  153.3 1.5 multiply_convert_fusion.1
  154.9 0.9 fusion.28
  156.6 1.9 %collective-permute-start.14 = (bf16[24,3,256]{2,1,0:T(4,128)(2,1)S(1)}, bf16[24,3,256]{2,1,0:T(4,128)(2,1)S(1)}, u32[]{:S(2)}, u32[]{:S(2)}) collective-permute-start(bf16[24,3,256]{2,1,0:T(4,128)(2,1)S(1)} %get-tuple-element.15), channel_id=1, source_target_pairs={{0,1},{1,2},{2,3},{3,4},{4,5},{5,6},{6,7},{7,8},{8,9},{9,10},{10,1... | collective-permute-start | bytes 110600 | tf_op jit(solution)/shard_map/ppermute | solution.py:27
  158.6 5.8 %collective-permute-start.15 = (bf16[24,3,256]{2,1,0:T(4,128)(2,1)S(1)}, bf16[24,3,256]{2,1,0:T(4,128)(2,1)S(1)}, u32[]{:S(2)}, u32[]{:S(2)}) collective-permute-start(bf16[24,3,256]{2,1,0:T(4,128)(2,1)S(1)} %get-tuple-element.16), channel_id=1, source_target_pairs={{1,0},{2,1},{3,2},{4,3},{5,4},{6,5},{7,6},{8,7},{9,8},{10,9},{11,1... | collective-permute-start | bytes 110600 | tf_op jit(solution)/shard_map/ppermute | solution.py:28
  164.3 1.7 collective-permute-done.15
  166.1 1.9 %collective-permute-start.16 = (bf16[3,30,256]{2,1,0:T(8,128)(2,1)S(1)}, bf16[3,30,256]{2,1,0:T(8,128)(2,1)S(1)}, u32[]{:S(2)}, u32[]{:S(2)}) collective-permute-start(bf16[3,30,256]{2,1,0:T(8,128)(2,1)S(1)} %get-tuple-element.11), channel_id=1, source_target_pairs={{0,48},{48,96},{96,144},{144,192},{192,240},{240,288},{288,336},{3... | collective-permute-start | bytes 138248 | tf_op jit(solution)/shard_map/ppermute | solution.py:27
  168.0 3.9 %collective-permute-start.17 = (bf16[3,30,256]{2,1,0:T(8,128)(2,1)S(1)}, bf16[3,30,256]{2,1,0:T(8,128)(2,1)S(1)}, u32[]{:S(2)}, u32[]{:S(2)}) collective-permute-start(bf16[3,30,256]{2,1,0:T(8,128)(2,1)S(1)} %get-tuple-element.12), channel_id=1, source_target_pairs={{48,0},{96,48},{144,96},{192,144},{240,192},{288,240},{336,288},{3... | collective-permute-start | bytes 138248 | tf_op jit(solution)/shard_map/ppermute | solution.py:28
  172.1 6.1 %collective-permute-done.17 = bf16[3,30,256]{2,1,0:T(8,128)(2,1)S(1)} collective-permute-done((bf16[3,30,256]{2,1,0:T(8,128)(2,1)S(1)}, bf16[3,30,256]{2,1,0:T(8,128)(2,1)S(1)}, u32[]{:S(2)}, u32[]{:S(2)}) %collective-permute-start.17) | collective-permute-done | bytes 46112 | tf_op jit(solution)/shard_map/ppermute | solution.py:28
  178.5 9.3 %fusion.93 = (f32[24,24]{1,0:T(8,128)S(1)}, f32[1,24,24,256]{3,0,2,1:T(1,128)S(1)}) fusion(f32[2,7,7,256]{3,0,2,1:T(2,128)S(1)} %copy-done.10, bf16[1,30,30,256]{3,2,1,0:T(8,128)(2,1)S(1)} %maximum_bitcast_fusion.1), kind=kOutput, calls=%fused_computation.140 | convolution fusion | flops 86851008 | bytes 1133824 | tf_op jit(solution)/shard_map/conv_general_dilated | solution.py:62
  188.1 1.5 multiply_convert_fusion
  189.6 0.9 fusion.36
  190.5 1.2 fusion.48
  (76 shorter events, 10.7 us)
Async XLA Ops:
  0.0 9.1 %copy-start = (bf16[3,3,256,256]{3,2,1,0:T(8,128)(2,1)S(1)}, bf16[3,3,256,256]{3,2,1,0:T(8,128)(2,1)}, u32[]{:S(2)}) copy-start(bf16[3,3,256,256]{3,2,1,0:T(8,128)(2,1)} %param.14) | copy-start | bytes 3538948
  5.5 3.3 %copy-start.7 = (s32[2,1]{0,1:T(1,128)S(1)}, s32[2,1]{0,1:T(1,128)}, u32[]{:S(2)}) copy-start(s32[2,1]{0,1:T(1,128)} %param.16) | copy-start | bytes 28
  5.5 3.6 %copy-start.11 = (f32[256]{0:T(256)S(1)}, f32[256]{0:T(256)}, u32[]{:S(2)}) copy-start(f32[256]{0:T(256)} %param.15) | copy-start | bytes 3076
  5.5 3.6 %copy-start.12 = (pred[16,5]{0,1:T(8,128)(4,1)S(1)}, pred[16,5]{0,1:T(8,128)(4,1)}, u32[]{:S(2)}) copy-start(pred[16,5]{0,1:T(8,128)(4,1)} %constant.51) | copy-start | bytes 244
  16.7 1.9 copy-start.5
  16.7 1.8 copy-start.6
  21.3 83.9 %collective-permute-start.6 = (bf16[2,32,32,256]{3,1,2,0:T(8,128)(2,1)S(1)}, bf16[2,32,32,256]{3,1,2,0:T(8,128)(2,1)}, u32[]{:S(2)}, u32[]{:S(2)}) collective-permute-start(bf16[2,32,32,256]{3,1,2,0:T(8,128)(2,1)S(1)} %copy.34), channel_id=1, source_target_pairs={{0,48},{48,96},{96,144},{144,192},{192,240},{240,288},{288,336},{3... | collective-permute-start | bytes 3145736 | tf_op jit(solution)/shard_map/ppermute | solution.py:17
  28.4 3.6 %copy-start.3 = (bf16[2,16,32]{2,1,0:T(8,128)(2,1)S(1)}, bf16[2,16,32]{2,1,0:T(8,128)(2,1)}, u32[]{:S(2)}) copy-start(bf16[2,16,32]{2,1,0:T(8,128)(2,1)} %param.19) | copy-start | bytes 6148
  28.4 23.5 %copy-start.2 = (bf16[2,16,32]{2,1,0:T(8,128)(2,1)S(1)}, bf16[2,16,32]{2,1,0:T(8,128)(2,1)}, u32[]{:S(2)}) copy-start(bf16[2,16,32]{2,1,0:T(8,128)(2,1)} %param.20) | copy-start | bytes 6148
  30.1 75.1 %collective-permute-start.7 = (bf16[2,32,32,256]{3,1,2,0:T(8,128)(2,1)}, bf16[2,32,32,256]{3,1,2,0:T(8,128)(2,1)}, u32[]{:S(2)}, u32[]{:S(2)}) collective-permute-start(bf16[2,32,32,256]{3,1,2,0:T(8,128)(2,1)} %copy.35), channel_id=1, source_target_pairs={{48,0},{96,48},{144,96},{192,144},{240,192},{288,240},{336,288},{3... | collective-permute-start | bytes 3145736 | tf_op jit(solution)/shard_map/ppermute | solution.py:17
  32.9 69.6 %collective-permute-start.4 = (bf16[2,16,32]{2,1,0:T(8,128)(2,1)}, bf16[2,16,32]{2,1,0:T(8,128)(2,1)}, u32[]{:S(2)}, u32[]{:S(2)}) collective-permute-start(bf16[2,16,32]{2,1,0:T(8,128)(2,1)} %reshape.188), channel_id=1, source_target_pairs={{0,48},{48,96},{96,144},{144,192},{192,240},{240,288},{288,336},{3... | collective-permute-start | bytes 6152 | tf_op jit(solution)/shard_map/ppermute | solution.py:17
  41.9 63.3 %collective-permute-start.5 = (bf16[2,16,32]{2,1,0:T(8,128)(2,1)}, bf16[2,16,32]{2,1,0:T(8,128)(2,1)}, u32[]{:S(2)}, u32[]{:S(2)}) collective-permute-start(bf16[2,16,32]{2,1,0:T(8,128)(2,1)} %reshape.189), channel_id=1, source_target_pairs={{48,0},{96,48},{144,96},{192,144},{240,192},{288,240},{336,288},{3... | collective-permute-start | bytes 6152 | tf_op jit(solution)/shard_map/ppermute | solution.py:17
  43.8 28.4 %collective-permute-start = (s32[2]{0:T(128)}, s32[2]{0:T(128)}, u32[]{:S(2)}, u32[]{:S(2)}) collective-permute-start(s32[2]{0:T(128)} %get-tuple-element.8), channel_id=1, source_target_pairs={{0,48},{48,96},{96,144},{144,192},{192,240},{240,288},{288,336},{3... | collective-permute-start | bytes 32 | tf_op jit(solution)/shard_map/ppermute | solution.py:17
  72.1 11.0 %collective-permute-start.1 = (s32[2]{0:T(128)}, s32[2]{0:T(128)S(1)}, u32[]{:S(2)}, u32[]{:S(2)}) collective-permute-start(s32[2]{0:T(128)} %get-tuple-element.7), channel_id=1, source_target_pairs={{48,0},{96,48},{144,96},{192,144},{240,192},{288,240},{336,288},{3... | collective-permute-start | bytes 32 | tf_op jit(solution)/shard_map/ppermute | solution.py:17
  83.2 5.5 %collective-permute-start.8 = (s32[2]{0:T(128)}, s32[2]{0:T(128)S(1)}, u32[]{:S(2)}, u32[]{:S(2)}) collective-permute-start(s32[2]{0:T(128)} %get-tuple-element.5), channel_id=1, source_target_pairs={{0,48},{48,96},{96,144},{144,192},{192,240},{240,288},{288,336},{3... | collective-permute-start | bytes 32 | tf_op jit(solution)/shard_map/ppermute | solution.py:17
  88.6 9.9 %collective-permute-start.9 = (s32[2]{0:T(128)}, s32[2]{0:T(128)S(1)}, u32[]{:S(2)}, u32[]{:S(2)}) collective-permute-start(s32[2]{0:T(128)} %get-tuple-element.6), channel_id=1, source_target_pairs={{48,0},{96,48},{144,96},{192,144},{240,192},{288,240},{336,288},{3... | collective-permute-start | bytes 32 | tf_op jit(solution)/shard_map/ppermute | solution.py:17
  98.5 8.9 %collective-permute-start.2 = (bf16[2,16,32]{2,1,0:T(8,128)(2,1)}, bf16[2,16,32]{2,1,0:T(8,128)(2,1)S(1)}, u32[]{:S(2)}, u32[]{:S(2)}) collective-permute-start(bf16[2,16,32]{2,1,0:T(8,128)(2,1)} %reshape.185), channel_id=1, source_target_pairs={{0,48},{48,96},{96,144},{144,192},{192,240},{240,288},{288,336},{3... | collective-permute-start | bytes 6152 | tf_op jit(solution)/shard_map/ppermute | solution.py:17
  102.6 10.0 %collective-permute-start.3 = (bf16[2,16,32]{2,1,0:T(8,128)(2,1)}, bf16[2,16,32]{2,1,0:T(8,128)(2,1)S(1)}, u32[]{:S(2)}, u32[]{:S(2)}) collective-permute-start(bf16[2,16,32]{2,1,0:T(8,128)(2,1)} %reshape.186), channel_id=1, source_target_pairs={{48,0},{96,48},{144,96},{192,144},{240,192},{288,240},{336,288},{3... | collective-permute-start | bytes 6152 | tf_op jit(solution)/shard_map/ppermute | solution.py:17
  107.4 9.0 %copy-start.1 = (bf16[24,24,256]{2,1,0:T(8,128)(2,1)S(1)}, bf16[24,24,256]{2,1,0:T(8,128)(2,1)}, u32[]{:S(2)}) copy-start(bf16[24,24,256]{2,1,0:T(8,128)(2,1)} %param.21) | copy-start | bytes 884740
  115.5 20.7 %copy-start.4 = (f32[2,256]{1,0:T(2,128)S(1)}, f32[2,256]{1,0:T(2,128)}, u32[]{:S(2)}) copy-start(f32[2,256]{1,0:T(2,128)} %param.23) | copy-start | bytes 6148
  115.5 28.2 %copy-start.10 = (f32[2,7,7,256]{3,0,2,1:T(2,128)S(1)}, f32[2,7,7,256]{3,0,2,1:T(2,128)}, u32[]{:S(2)}) copy-start(f32[2,7,7,256]{3,0,2,1:T(2,128)} %param.22) | copy-start | bytes 301060
  116.9 11.5 %collective-permute-start.10 = (bf16[24,3,256]{2,1,0:T(4,128)(2,1)S(1)}, bf16[24,3,256]{2,1,0:T(4,128)(2,1)S(1)}, u32[]{:S(2)}, u32[]{:S(2)}) collective-permute-start(bf16[24,3,256]{2,1,0:T(4,128)(2,1)S(1)} %get-tuple-element.17), channel_id=1, source_target_pairs={{0,1},{1,2},{2,3},{3,4},{4,5},{5,6},{6,7},{7,8},{8,9},{9,10},{10,1... | collective-permute-start | bytes 110600 | tf_op jit(solution)/shard_map/ppermute | solution.py:27
  118.8 11.3 %collective-permute-start.11 = (bf16[24,3,256]{2,1,0:T(4,128)(2,1)S(1)}, bf16[24,3,256]{2,1,0:T(4,128)(2,1)S(1)}, u32[]{:S(2)}, u32[]{:S(2)}) collective-permute-start(bf16[24,3,256]{2,1,0:T(4,128)(2,1)S(1)} %get-tuple-element.18), channel_id=1, source_target_pairs={{1,0},{2,1},{3,2},{4,3},{5,4},{6,5},{7,6},{8,7},{9,8},{10,9},{11,1... | collective-permute-start | bytes 110600 | tf_op jit(solution)/shard_map/ppermute | solution.py:28
  130.1 6.1 %collective-permute-start.12 = (bf16[3,30,256]{2,1,0:T(8,128)(2,1)S(1)}, bf16[3,30,256]{2,1,0:T(8,128)(2,1)S(1)}, u32[]{:S(2)}, u32[]{:S(2)}) collective-permute-start(bf16[3,30,256]{2,1,0:T(8,128)(2,1)S(1)} %get-tuple-element.13), channel_id=1, source_target_pairs={{0,48},{48,96},{96,144},{144,192},{192,240},{240,288},{288,336},{3... | collective-permute-start | bytes 138248 | tf_op jit(solution)/shard_map/ppermute | solution.py:27
  133.3 10.2 %collective-permute-start.13 = (bf16[3,30,256]{2,1,0:T(8,128)(2,1)S(1)}, bf16[3,30,256]{2,1,0:T(8,128)(2,1)S(1)}, u32[]{:S(2)}, u32[]{:S(2)}) collective-permute-start(bf16[3,30,256]{2,1,0:T(8,128)(2,1)S(1)} %get-tuple-element.14), channel_id=1, source_target_pairs={{48,0},{96,48},{144,96},{192,144},{240,192},{288,240},{336,288},{3... | collective-permute-start | bytes 138248 | tf_op jit(solution)/shard_map/ppermute | solution.py:28
  153.0 1.9 copy-start.8
  154.9 1.2 copy-start.9
  156.6 7.7 %collective-permute-start.14 = (bf16[24,3,256]{2,1,0:T(4,128)(2,1)S(1)}, bf16[24,3,256]{2,1,0:T(4,128)(2,1)S(1)}, u32[]{:S(2)}, u32[]{:S(2)}) collective-permute-start(bf16[24,3,256]{2,1,0:T(4,128)(2,1)S(1)} %get-tuple-element.15), channel_id=1, source_target_pairs={{0,1},{1,2},{2,3},{3,4},{4,5},{5,6},{6,7},{7,8},{8,9},{9,10},{10,1... | collective-permute-start | bytes 110600 | tf_op jit(solution)/shard_map/ppermute | solution.py:27
  158.6 7.5 %collective-permute-start.15 = (bf16[24,3,256]{2,1,0:T(4,128)(2,1)S(1)}, bf16[24,3,256]{2,1,0:T(4,128)(2,1)S(1)}, u32[]{:S(2)}, u32[]{:S(2)}) collective-permute-start(bf16[24,3,256]{2,1,0:T(4,128)(2,1)S(1)} %get-tuple-element.16), channel_id=1, source_target_pairs={{1,0},{2,1},{3,2},{4,3},{5,4},{6,5},{7,6},{8,7},{9,8},{10,9},{11,1... | collective-permute-start | bytes 110600 | tf_op jit(solution)/shard_map/ppermute | solution.py:28
  166.1 6.0 %collective-permute-start.16 = (bf16[3,30,256]{2,1,0:T(8,128)(2,1)S(1)}, bf16[3,30,256]{2,1,0:T(8,128)(2,1)S(1)}, u32[]{:S(2)}, u32[]{:S(2)}) collective-permute-start(bf16[3,30,256]{2,1,0:T(8,128)(2,1)S(1)} %get-tuple-element.11), channel_id=1, source_target_pairs={{0,48},{48,96},{96,144},{144,192},{192,240},{240,288},{288,336},{3... | collective-permute-start | bytes 138248 | tf_op jit(solution)/shard_map/ppermute | solution.py:27
  168.0 10.2 %collective-permute-start.17 = (bf16[3,30,256]{2,1,0:T(8,128)(2,1)S(1)}, bf16[3,30,256]{2,1,0:T(8,128)(2,1)S(1)}, u32[]{:S(2)}, u32[]{:S(2)}) collective-permute-start(bf16[3,30,256]{2,1,0:T(8,128)(2,1)S(1)} %get-tuple-element.12), channel_id=1, source_target_pairs={{48,0},{96,48},{144,96},{192,144},{240,192},{288,240},{336,288},{3... | collective-permute-start | bytes 138248 | tf_op jit(solution)/shard_map/ppermute | solution.py:28
where the time goes:
time: 192 us
  starting transfers between devices  69.9 us (36%)
  waiting for transfers between devices  54.9 us (29%)
  matrix products  39.7 us (21%)
  local copies, waits for them, and re-layouts  16.9 us (9%)
  other arithmetic  9.81 us (5%)
    ppermute x10, starting transfers between devices, shifted(): lax.ppermute(value, axis, [(source, source + steps) for source in range(l...  38.8 us
    ppermute x10, waiting for transfers between devices, shifted(): lax.ppermute(value, axis, [(source, source + steps) for source in range(l...  37.9 us
    ppermute x4, starting transfers between devices, with_halo(): after = lax.ppermute(leading, axis, down)  22.2 us
    conv_general_dilated x2, matrix products, layer_apply(): lax.conv_general_dilated(widened[None], kernel, (1, 1), ((0, 0), (0, 0)),...  18.5 us
    ppermute x4, waiting for transfers between devices, with_halo(): after = lax.ppermute(leading, axis, down)  16.8 us
    ppermute x4, starting transfers between devices, with_halo(): before = lax.ppermute(last, axis, up)  8.93 us
    unnamed x33, local copies, waits for them, and re-layouts  7.19 us
    conv_general_dilated x1, matrix products, per_device(): lax.conv_general_dilated(swath_input, conv_weight, (2, 2), ((1, 1), (1, 1...  7.11 us
  transfers between devices with their start and end apart: 18, of which 10 were waited for; matrix products, arithmetic and copies ran while one was open for 7% of the time, Pallas kernels for 0%

commit v1 on v0

v1 whole, which is shorter than its diff:
```python
import functools

import jax
import jax.numpy as jnp
import numpy as np
from jax import lax
from jax.experimental import pallas as pl
from jax.experimental.pallas import tpu as pltpu
from jax.sharding import PartitionSpec as P

KS = 7
HALO = 3
LAYERS = 2
NB = 2
OB = 32
IB = 64
RB = 16
T = 24
CELLS = T * T
C = 256
HID = 1024
STRIP = 112
F32 = jnp.float32
BF16 = jnp.bfloat16
MESH = pl.DeviceIdType.MESH
DIAGS = ((1, 0), (-1, 0), (0, 1), (0, -1), (1, 1), (-1, 1), (1, -1), (-1, -1))


def strip_source(first_col):
    cells = np.full((STRIP,), -1)
    for k in range(9):
        cells[k] = (T - HALO + k // 3) * T + first_col + k % 3
        cells[96 + k] = (k // 3) * T + first_col + k % 3
    for k in range(3 * T):
        cells[16 + k] = (k // 3) * T + first_col + k % 3
    return cells


def pick_matrix(first_col):
    return (strip_source(first_col)[:, None] == np.arange(CELLS)[None, :]).astype(np.float32)


def spread_matrix(first):
    out = np.zeros((30 * 8, STRIP), np.float32)
    for y in range(30):
        base = y * 3 if y < 3 else (16 + (y - 3) * 3 if y < 27 else 96 + (y - 27) * 3)
        for t in range(3):
            out[y * 8 + first + t, base + t] = 1
    return out


def gelu(x):
    inner = x * (0.7978845608028654 + 0.035677408136300125 * (x * x))
    half = 0.5 * x
    return half + half * jnp.tanh(inner)


def body(
    nlat, nlon,
    band, roff, coff, swath, wconv, bias, roww, colw, back, depth, gain, up, down,
    pick_l, pick_r, spread_l, spread_r,
    out,
    x_s, w_s, up_s, dn_s, t_s, x3_s, feat_s, kron_s, own_s, north_s, south_s,
    meta_s, meta_n, meta_d, onehot_s, acc_s, st_s, pad_s, mix_s,
    edge_l, edge_r, strip_l, strip_r, top_s, bot_s,
    load_sem, bsend, brecv, msend, mrecv, hsend, hrecv,
):
    lat, lon = lax.axis_index("lat"), lax.axis_index("lon")

    def at(dlat, dlon):
        return (lax.rem(lat + dlat + nlat, nlat), lax.rem(lon + dlon + nlon, nlon))

    barrier = pltpu.get_barrier_semaphore()
    for d in DIAGS:
        pl.semaphore_signal(barrier, inc=1, device_id=at(*d), device_id_type=MESH)

    loads = [
        pltpu.make_async_copy(swath.at[0], x_s.at[0], load_sem.at[0]),
        pltpu.make_async_copy(wconv, w_s, load_sem.at[2]),
        pltpu.make_async_copy(swath.at[1], x_s.at[1], load_sem.at[1]),
        pltpu.make_async_copy(up, up_s, load_sem.at[3]),
        pltpu.make_async_copy(down, dn_s, load_sem.at[4]),
    ]
    for cp in loads:
        cp.start()

    row8 = lax.broadcasted_iota(jnp.int32, (8, C), 0)

    def codes(target):
        c0 = jnp.where(band[0, 0] == target, roff[0] * 64 + coff[0], -4096)
        c1 = jnp.where(band[1, 0] == target, roff[1] * 64 + coff[1], -4096)
        return jnp.where(row8 == 0, c0, jnp.where(row8 == 1, c1, -4096))

    meta_s[0] = codes(lat)
    meta_s[1] = codes(lat - 1)
    meta_s[2] = codes(lat + 1)

    cell = lax.broadcasted_iota(jnp.int32, (CELLS, C), 0)
    pos = lax.broadcasted_iota(jnp.int32, (CELLS, C), 1)
    h = (cell * 2731) >> 16
    w = cell - h * T
    diff = (h - (pos >> 4)) * 64 + (w - (pos & 15))
    acc_s[...] = diff

    def build_onehot(slot, meta_ref):
        for s in range(NB):
            code = meta_ref[s:s + 1, :]
            onehot_s[2 * slot + s] = jnp.where(acc_s[...] == code, 1.0, 0.0).astype(BF16)

    build_onehot(0, meta_s.at[0])

    m_i = lax.broadcasted_iota(jnp.int32, (RB * RB, RB), 0)
    r_i = lax.broadcasted_iota(jnp.int32, (RB * RB, RB), 1)
    exp_r = jnp.where((m_i >> 4) == r_i, 1.0, 0.0).astype(BF16)
    exp_u = jnp.where((m_i & 15) == r_i, 1.0, 0.0).astype(BF16)
    k_i = lax.broadcasted_iota(jnp.int32, (OB, OB * OB), 1)
    i_i = lax.broadcasted_iota(jnp.int32, (OB, OB * OB), 0)
    exp_i = jnp.where((k_i >> 5) == i_i, 1.0, 0.0).astype(BF16)
    exp_j = jnp.where((k_i & 31) == i_i, 1.0, 0.0).astype(BF16)
    for b in range(NB):
        rows = jnp.dot(exp_r, roww[b], preferred_element_type=F32).astype(BF16)
        cols = jnp.dot(exp_u, colw[b], preferred_element_type=F32).astype(BF16)
        for q in range(4):
            part = slice(q * 256, (q + 1) * 256)
            left = jnp.dot(rows, exp_i[:, part], preferred_element_type=F32)
            right = jnp.dot(cols, exp_j[:, part], preferred_element_type=F32)
            kron_s[b, :, part] = (left * right).astype(BF16)

    t_s[:, :, 0:8, :] = jnp.zeros((2, 8, 8, 128), F32)
    x3_s[0, 0] = jnp.zeros((OB, 3 * C), BF16)

    pl.semaphore_wait(barrier, len(DIAGS))
    metas = [
        pltpu.make_async_remote_copy(meta_s.at[1], meta_d, msend.at[0], mrecv.at[0], device_id=at(-1, 0), device_id_type=MESH),
        pltpu.make_async_remote_copy(meta_s.at[2], meta_n, msend.at[1], mrecv.at[1], device_id=at(1, 0), device_id_type=MESH),
    ]
    for cp in metas:
        cp.start()

    sends = []
    for b in range(NB):
        loads[0 if b == 0 else 2].wait()
        if b == 0:
            loads[1].wait()

        def spread_rows(g, _, b=b):
            for k in range(8):
                r = g * 8 + k
                for c in range(2):
                    t_s[c, k, 8:72, :] = x_s[b, r, :, c * 128:(c + 1) * 128].astype(F32)
            for k in range(8):
                hi, lo = (k + 1) // 2, (k + 1) % 2
                for e in range(3):
                    for c in range(2):
                        piece = t_s[c, k, pl.ds(7 + e, OB, stride=2), :].astype(BF16)
                        x3_s[g * 4 + hi, lo, :, e * C + c * 128:e * C + (c + 1) * 128] = piece
            return 0

        lax.fori_loop(0, 8, spread_rows, 0)

        def conv_rows(g, _):
            i0 = g * 8
            total = jnp.dot(x3_s[pl.ds(i0, 8), 0].reshape(256, 3 * C), w_s[0], preferred_element_type=F32)
            total += jnp.dot(x3_s[pl.ds(i0, 8), 1].reshape(256, 3 * C), w_s[1], preferred_element_type=F32)
            total += jnp.dot(x3_s[pl.ds(i0 + 1, 8), 0].reshape(256, 3 * C), w_s[2], preferred_element_type=F32)
            feat_s[pl.ds(pl.multiple_of(g * 256, 256), 256), :] = gelu(total + bias[...]).astype(BF16)
            return 0

        lax.fori_loop(0, 4, conv_rows, 0)
        own_s[b] = jnp.dot(kron_s[b], feat_s[...], preferred_element_type=F32).astype(BF16)
        pair = [
            pltpu.make_async_remote_copy(own_s.at[b], south_s.at[b], bsend.at[b, 0], brecv.at[b, 0], device_id=at(-1, 0), device_id_type=MESH),
            pltpu.make_async_remote_copy(own_s.at[b], north_s.at[b], bsend.at[b, 1], brecv.at[b, 1], device_id=at(1, 0), device_id_type=MESH),
        ]
        for cp in pair:
            cp.start()
        sends.append(pair)

    for cp in metas:
        cp.wait()
    build_onehot(1, meta_n)
    build_onehot(2, meta_d)

    for b in range(NB):
        for cp in sends[b]:
            cp.wait()
    for q in range(3):
        part = slice(q * 192, (q + 1) * 192)
        total = back[part, :].astype(F32)
        for b in range(NB):
            total += jnp.dot(onehot_s[b, part, :], own_s[b], preferred_element_type=F32)
            total += jnp.dot(onehot_s[2 + b, part, :], north_s[b], preferred_element_type=F32)
            total += jnp.dot(onehot_s[4 + b, part, :], south_s[b], preferred_element_type=F32)
        st_s[0, part, :] = total.astype(BF16)

    loads[3].wait()
    loads[4].wait()

    has_top = jnp.where(lat > 0, 1.0, 0.0).astype(F32)
    has_bot = jnp.where(lat < nlat - 1, 1.0, 0.0).astype(F32)

    for l in range(LAYERS):
        st = st_s.at[l]
        edge_l[l] = jnp.dot(pick_l[...], st[...], preferred_element_type=F32).astype(BF16)
        edge_r[l] = jnp.dot(pick_r[...], st[...], preferred_element_type=F32).astype(BF16)
        moves = [
            (st.at[pl.ds(496, 80)], bot_dst(top_s, l), (1, 0)),
            (st.at[pl.ds(0, 80)], bot_dst(bot_s, l), (-1, 0)),
            (edge_r.at[l, pl.ds(16, 80)], strip_l.at[l, pl.ds(16, 80)], (0, 1)),
            (edge_l.at[l, pl.ds(16, 80)], strip_r.at[l, pl.ds(16, 80)], (0, -1)),
            (edge_r.at[l, pl.ds(0, 16)], strip_l.at[l, pl.ds(0, 16)], (1, 1)),
            (edge_r.at[l, pl.ds(96, 16)], strip_l.at[l, pl.ds(96, 16)], (-1, 1)),
            (edge_l.at[l, pl.ds(0, 16)], strip_r.at[l, pl.ds(0, 16)], (1, -1)),
            (edge_l.at[l, pl.ds(96, 16)], strip_r.at[l, pl.ds(96, 16)], (-1, -1)),
        ]
        copies = [
            pltpu.make_async_remote_copy(src, dst, hsend.at[l, n], hrecv.at[l, n], device_id=at(*d), device_id_type=MESH)
            for n, (src, dst, d) in enumerate(moves)
        ]
        for cp in copies:
            cp.start()
        for c in range(2):
            lanes = slice(c * 128, (c + 1) * 128)
            pad_s[c, 3:27, 8:32, :] = st[:, lanes].astype(F32).reshape(T, T, 128)
        for cp in copies:
            cp.wait()
        left = jnp.dot(spread_l[...], strip_l[l], preferred_element_type=F32).reshape(30, 8, C)
        right = jnp.dot(spread_r[...], strip_r[l], preferred_element_type=F32).reshape(30, 8, C)
        upper = top_s[l].astype(F32)[8:80].reshape(3, T, C) * has_top
        lower = bot_s[l].astype(F32)[0:72].reshape(3, T, C) * has_bot
        for c in range(2):
            lanes = slice(c * 128, (c + 1) * 128)
            for side, lo in ((left, 0), (right, 32)):
                pad_s[c, 0:3, lo:lo + 8, :] = side[0:3, :, lanes] * has_top
                pad_s[c, 3:27, lo:lo + 8, :] = side[3:27, :, lanes]
                pad_s[c, 27:30, lo:lo + 8, :] = side[27:30, :, lanes] * has_bot
            pad_s[c, 0:3, 8:32, :] = upper[:, :, lanes]
            pad_s[c, 27:30, 8:32, :] = lower[:, :, lanes]

        def mix_rows(g, _, l=l):
            c, h0 = g // 3, (g % 3) * 8
            acc = [None] * 8
            for e in range(KS):
                wt = [depth[l, a, e, pl.ds(c, 1), :] for a in range(KS)]
                for r in range(14):
                    line = pad_s[c, h0 + r, 5 + e:29 + e, :]
                    for a in range(KS):
                        o = r - a
                        if 0 <= o < 8:
                            term = line * wt[a]
                            acc[o] = term if acc[o] is None else acc[o] + term
            for o in range(8):
                mix_s[c, h0 + o] = acc[o]
            return 0

        lax.fori_loop(0, 6, mix_rows, 0)

        def cells_step(g, _, l=l, st=st):
            m0 = mix_s[0, pl.ds(g * 8, 8)].reshape(192, 128)
            m1 = mix_s[1, pl.ds(g * 8, 8)].reshape(192, 128)
            mean = jnp.sum(m0 + m1, axis=-1, keepdims=True) * (1.0 / C)
            c0, c1 = m0 - mean, m1 - mean
            var = jnp.sum(c0 * c0 + c1 * c1, axis=-1, keepdims=True) * (1.0 / C)
            inv = lax.rsqrt(var + 1e-6)
            normed = jnp.concatenate(
                [(c0 * inv * gain[l:l + 1, 0:128]).astype(BF16), (c1 * inv * gain[l:l + 1, 128:256]).astype(BF16)], axis=1
            )
            hid = gelu(jnp.dot(normed, up_s[l], preferred_element_type=F32)).astype(BF16)
            part = pl.ds(pl.multiple_of(g * 192, 192), 192)
            new = st[part, :].astype(F32) + jnp.dot(hid, dn_s[l], preferred_element_type=F32)
            if l == LAYERS - 1:
                out[part, :] = new.astype(BF16)
            else:
                st_s[l + 1, part, :] = new.astype(BF16)
            return 0

        lax.fori_loop(0, 3, cells_step, 0)


def bot_dst(ref, l):
    return ref.at[l]


def solution(mesh):
    nlat, nlon = mesh.shape["lat"], mesh.shape["lon"]

    def per_device(swath, wconv, bias, band, roff, coff, roww, colw, back, depth, gain, up, down):
        smem = pl.BlockSpec(memory_space=pltpu.SMEM)
        vmem = pl.BlockSpec(memory_space=pltpu.VMEM)
        hbm = pl.BlockSpec(memory_space=pl.ANY)
        dma = pltpu.SemaphoreType.DMA
        result = pl.pallas_call(
            functools.partial(body, nlat, nlon),
            out_shape=jax.ShapeDtypeStruct((CELLS, C), BF16),
            in_specs=[smem, smem, smem, hbm, hbm] + [vmem] * 6 + [hbm, hbm] + [vmem] * 4,
            out_specs=vmem,
            scratch_shapes=[
                pltpu.VMEM((NB, IB, IB, C), BF16),
                pltpu.VMEM((3, 3 * C, C), BF16),
                pltpu.VMEM((LAYERS, C, HID), BF16),
                pltpu.VMEM((LAYERS, HID, C), BF16),
                pltpu.VMEM((2, 8, 72, 128), F32),
                pltpu.VMEM((33, 2, OB, 3 * C), BF16),
                pltpu.VMEM((OB * OB, C), BF16),
                pltpu.VMEM((NB, RB * RB, OB * OB), BF16),
                pltpu.VMEM((NB, RB * RB, C), BF16),
                pltpu.VMEM((NB, RB * RB, C), BF16),
                pltpu.VMEM((NB, RB * RB, C), BF16),
                pltpu.VMEM((3, 8, C), jnp.int32),
                pltpu.VMEM((8, C), jnp.int32),
                pltpu.VMEM((8, C), jnp.int32),
                pltpu.VMEM((3 * NB, CELLS, RB * RB), BF16),
                pltpu.VMEM((CELLS, C), jnp.int32),
                pltpu.VMEM((LAYERS, CELLS, C), BF16),
                pltpu.VMEM((2, 30, 40, 128), F32),
                pltpu.VMEM((2, T, T, 128), F32),
                pltpu.VMEM((LAYERS, STRIP, C), BF16),
                pltpu.VMEM((LAYERS, STRIP, C), BF16),
                pltpu.VMEM((LAYERS, STRIP, C), BF16),
                pltpu.VMEM((LAYERS, STRIP, C), BF16),
                pltpu.VMEM((LAYERS, 80, C), BF16),
                pltpu.VMEM((LAYERS, 80, C), BF16),
                dma((5,)),
                dma((NB, 2)),
                dma((NB, 2)),
                dma((2,)),
                dma((2,)),
                dma((LAYERS, 8)),
                dma((LAYERS, 8)),
            ],
            compiler_params=pltpu.CompilerParams(
                collective_id=0, has_side_effects=True, vmem_limit_bytes=56 * 1024 * 1024
            ),
        )(
            band, roff, coff, swath, wconv.reshape(3, 3 * C, C), bias.reshape(1, C), roww, colw,
            back.reshape(CELLS, C), depth.reshape(LAYERS, KS, KS, 2, 128), gain, up, down,
            jnp.asarray(pick_matrix(0), BF16), jnp.asarray(pick_matrix(T - HALO), BF16),
            jnp.asarray(spread_matrix(5), BF16), jnp.asarray(spread_matrix(0), BF16),
        )
        return result.reshape(T, T, C)

    split = P(("lat", "lon"))
    in_specs = (split, P(), P(), split, split, split, split, split, P("lat", "lon"), P(), P(), P(), P())
    return jax.shard_map(
        per_device, mesh=mesh, in_specs=in_specs, out_specs=P("lat", "lon", None), check_vma=False
    )
```

time: 192 us -> 63.7 us (0.33)
  the two profiles are of different devices: /device:TPU:22 before, /device:TPU:1 now
where the time goes in v1:
time: 63.7 us; the launch traced here: 63.4 us
  Pallas kernels  58.7 us (92%)
  local copies, waits for them, and re-layouts  4.69 us (7%)
    pallas_call x1, Pallas kernels, per_device(): pl.pallas_call(functools.partial(body, nlat, nlon), out_shape=jax.ShapeDt...  58.7 us
    unnamed x2, local copies, waits for them, and re-layouts  3.01 us
    reshape x2, local copies, waits for them, and re-layouts, per_device(): depth.reshape(LAYERS, KS, KS, 2, 128)  1.69 us

profile of v1, /device:TPU:1, one launch (start us, length us, event | category | flops | bytes accessed | tf_op | source)
XLA Modules:
  0.0 63.4 jit_solution(13657663131712355323)
XLA Ops:
  0.0 1.3 %copy.20.band = s32[2,1]{1,0:T(2,128)} copy(s32[2,1]{0,1:T(1,128)} %param.20) | data formatting | bytes 16 | tf_op args[3]
  1.3 1.0 %reshape.18 = f32[2,7,7,2,128]{4,3,0,2,1:T(2,128)S(1)} reshape(f32[2,7,7,256]{3,0,2,1:T(2,128)} %param.26) | data formatting | bytes 200704 | tf_op jit(solution)/shard_map/reshape | solution.py:336
  2.3 0.7 %copy.21.depth = f32[2,7,7,2,128]{4,3,2,1,0:T(2,128)} copy(f32[2,7,7,2,128]{4,3,0,2,1:T(2,128)S(1)} %reshape.18) | data formatting | bytes 200704 | tf_op jit(solution)/shard_map/reshape | solution.py:336
  3.0 58.7 %shard_map.163 = bf16[576,256]{1,0:T(8,128)(2,1)} custom-call(s32[2,1]{1,0:T(2,128)} %copy.20.band, s32[2]{0:T(128)} %roff.1, s32[2]{0:T(128)} %coff.1, bf16[2,64,64,256]{3,2,1,0:T(8,128)(2,1)} %swath.1, bf16[3,768,256]{2,1,0:T(8,128)(2,1)} %bitcast.6, f32[1,256]{1,0:T(1,128)} %bitcast.9, bf16[2,16,32]{2,1,0:T(8,128)(2,1)} %roww.1, bf16[2,16,32]{2,1,0:T(8,128)(2,1)} %colw.1, ...), custom_call_target="tpu_custom_call" | custom-call | tf_op jit(solution)/shard_map/pallas_call | solution.py:292
  61.7 1.7 %copy.23 = bf16[24,24,256]{2,1,0:T(8,128)(2,1)} copy(bf16[24,24,256]{2,1,0:T(8,128)(2,1)} %bitcast.7) | data formatting | bytes 589824

commit v2 on v1

v2 whole, which is shorter than its diff:
```python
import functools

import jax
import jax.numpy as jnp
import numpy as np
from jax import lax
from jax.experimental import pallas as pl
from jax.experimental.pallas import tpu as pltpu
from jax.sharding import PartitionSpec as P

KS = 7
HALO = 3
LAYERS = 2
NB = 2
OB = 32
IB = 64
RB = 16
T = 24
CELLS = T * T
C = 256
HID = 1024
SLOTS = 2
STRIP = 112
F32 = jnp.float32
BF16 = jnp.bfloat16
MESH = pl.DeviceIdType.MESH
DIAGS = ((1, 0), (-1, 0), (0, 1), (0, -1), (1, 1), (-1, 1), (1, -1), (-1, -1))


def strip_source(first_col):
    cells = np.full((STRIP,), -1)
    for k in range(9):
        cells[k] = (T - HALO + k // 3) * T + first_col + k % 3
        cells[96 + k] = (k // 3) * T + first_col + k % 3
    for k in range(3 * T):
        cells[16 + k] = (k // 3) * T + first_col + k % 3
    return cells


def pick_matrix(first_col):
    return (strip_source(first_col)[:, None] == np.arange(CELLS)[None, :]).astype(np.float32)


def spread_matrix(first):
    out = np.zeros((30 * 8, STRIP), np.float32)
    for y in range(30):
        base = y * 3 if y < 3 else (16 + (y - 3) * 3 if y < 27 else 96 + (y - 27) * 3)
        for t in range(3):
            out[y * 8 + first + t, base + t] = 1
    return out


def gelu(x):
    inner = x * (0.7978845608028654 + 0.035677408136300125 * (x * x))
    half = 0.5 * x
    return half + half * jnp.tanh(inner)


def body(
    nlat, nlon,
    band, roff, coff, swath, wconv, bias, roww, colw, back, depth, gain, up, down,
    pick_l, pick_r, spread_l, spread_r,
    out,
    x_s, w_s, up_s, dn_s, t_s, x3_s, feat_s, kron_s, own_s, north_s, south_s,
    meta_s, meta_n, meta_d, onehot_s, acc_s, sum_s, st_s, pad_s, mix_s,
    edge_l, edge_r, strip_l, strip_r, top_s, bot_s,
    roww_s, colw_s, bias_s, back_s, pick_ls, pick_rs, spread_ls, spread_rs, dep_s, gain_s,
    load_sem, bsend, brecv, msend, mrecv, hsend, hrecv,
):
    lat, lon = lax.axis_index("lat"), lax.axis_index("lon")

    def at(dlat, dlon):
        return (lax.rem(lat + dlat + nlat, nlat), lax.rem(lon + dlon + nlon, nlon))

    barrier = pltpu.get_barrier_semaphore()
    for d in DIAGS:
        pl.semaphore_signal(barrier, inc=1, device_id=at(*d), device_id_type=MESH)

    loads = [
        pltpu.make_async_copy(src, dst, load_sem.at[n])
        for n, (src, dst) in enumerate((
            (roww, roww_s), (colw, colw_s), (swath.at[0], x_s.at[0]), (bias, bias_s), (wconv, w_s), (swath.at[1], x_s.at[1]),
            (back, back_s), (pick_l, pick_ls), (pick_r, pick_rs), (spread_l, spread_ls), (spread_r, spread_rs),
            (depth, dep_s), (gain, gain_s), (up, up_s), (down, dn_s),
        ))
    ]
    for cp in loads:
        cp.start()

    row8 = lax.broadcasted_iota(jnp.int32, (8, C), 0)

    def codes(target):
        c0 = jnp.where(band[0] == target, roff[0] * 64 + coff[0], -4096)
        c1 = jnp.where(band[1] == target, roff[1] * 64 + coff[1], -4096)
        return jnp.where(row8 == 0, c0, jnp.where(row8 == 1, c1, -4096))

    meta_s[0] = codes(lat)
    meta_s[1] = codes(lat - 1)
    meta_s[2] = codes(lat + 1)

    cell = lax.broadcasted_iota(jnp.int32, (CELLS, C), 0)
    pos = lax.broadcasted_iota(jnp.int32, (CELLS, C), 1)
    h = (cell * 2731) >> 16
    w = cell - h * T
    diff = (h - (pos >> 4)) * 64 + (w - (pos & 15))
    acc_s[...] = diff

    def build_onehot(slot, meta_ref):
        for s in range(NB):
            code = meta_ref[s:s + 1, :]
            onehot_s[2 * slot + s] = jnp.where(acc_s[...] == code, 1.0, 0.0).astype(BF16)

    build_onehot(0, meta_s.at[0])

    m_i = lax.broadcasted_iota(jnp.int32, (RB * RB, RB), 0)
    r_i = lax.broadcasted_iota(jnp.int32, (RB * RB, RB), 1)
    exp_r = jnp.where((m_i >> 4) == r_i, 1.0, 0.0).astype(BF16)
    exp_u = jnp.where((m_i & 15) == r_i, 1.0, 0.0).astype(BF16)
    k_i = lax.broadcasted_iota(jnp.int32, (OB, OB * OB), 1)
    i_i = lax.broadcasted_iota(jnp.int32, (OB, OB * OB), 0)
    exp_i = jnp.where((k_i >> 5) == i_i, 1.0, 0.0).astype(BF16)
    exp_j = jnp.where((k_i & 31) == i_i, 1.0, 0.0).astype(BF16)
    loads[0].wait()
    loads[1].wait()
    for b in range(NB):
        rows = jnp.dot(exp_r, roww_s[b], preferred_element_type=F32).astype(BF16)
        cols = jnp.dot(exp_u, colw_s[b], preferred_element_type=F32).astype(BF16)
        for q in range(4):
            part = slice(q * 256, (q + 1) * 256)
            left = jnp.dot(rows, exp_i[:, part], preferred_element_type=F32)
            right = jnp.dot(cols, exp_j[:, part], preferred_element_type=F32)
            kron_s[b, :, part] = (left * right).astype(BF16)

    t_s[:, :, :, 0:8, :] = jnp.zeros((SLOTS, 2, 8, 8, 128), F32)
    x3_s[0, 0] = jnp.zeros((OB, 3 * C), BF16)

    sends = []
    for b in range(NB):
        loads[2 if b == 0 else 5].wait()
        if b == 0:
            loads[3].wait()
            loads[4].wait()

        def spread_rows(g, b=b):
            slot = g % SLOTS
            for k in range(8):
                for c in range(2):
                    t_s[slot, c, k, 8:72, :] = x_s[b, g * 8 + k, :, c * 128:(c + 1) * 128].astype(F32)
            for k in range(8):
                hi, lo = (k + 1) // 2, (k + 1) % 2
                for e in range(3):
                    for c in range(2):
                        piece = t_s[slot, c, k, pl.ds(7 + e, OB, stride=2), :].astype(BF16)
                        x3_s[g * 4 + hi, lo, :, e * C + c * 128:e * C + (c + 1) * 128] = piece

        def conv_rows(g):
            i0 = g * 8
            total = jnp.dot(x3_s[i0:i0 + 8, 0].reshape(256, 3 * C), w_s[0], preferred_element_type=F32)
            total += jnp.dot(x3_s[i0:i0 + 8, 1].reshape(256, 3 * C), w_s[1], preferred_element_type=F32)
            total += jnp.dot(x3_s[i0 + 1:i0 + 9, 0].reshape(256, 3 * C), w_s[2], preferred_element_type=F32)
            feat_s[g * 256:(g + 1) * 256, :] = gelu(total + bias_s[...]).astype(BF16)

        spread_rows(0)
        spread_rows(1)
        for g in range(4):
            if g < 3:
                spread_rows(2 * g + 2)
                spread_rows(2 * g + 3)
            conv_rows(g)
        own_s[b] = jnp.dot(kron_s[b], feat_s[...], preferred_element_type=F32).astype(BF16)
        if b == 0:
            pl.semaphore_wait(barrier, len(DIAGS))
            metas = [
                pltpu.make_async_remote_copy(meta_s.at[1], meta_d, msend.at[0], mrecv.at[0], device_id=at(-1, 0), device_id_type=MESH),
                pltpu.make_async_remote_copy(meta_s.at[2], meta_n, msend.at[1], mrecv.at[1], device_id=at(1, 0), device_id_type=MESH),
            ]
            for cp in metas:
                cp.start()
        pair = [
            pltpu.make_async_remote_copy(own_s.at[b], south_s.at[b], bsend.at[b, 0], brecv.at[b, 0], device_id=at(-1, 0), device_id_type=MESH),
            pltpu.make_async_remote_copy(own_s.at[b], north_s.at[b], bsend.at[b, 1], brecv.at[b, 1], device_id=at(1, 0), device_id_type=MESH),
        ]
        for cp in pair:
            cp.start()
        sends.append(pair)

    loads[6].wait()
    for cp in metas:
        cp.wait()
    build_onehot(1, meta_n)
    build_onehot(2, meta_d)

    for b in range(NB):
        for cp in sends[b]:
            cp.wait()
        for q in range(3):
            part = slice(q * 192, (q + 1) * 192)
            if b == 0:
                total = back_s[part, :].astype(F32)
                for k in range(NB):
                    total += jnp.dot(onehot_s[k, part, :], own_s[k], preferred_element_type=F32)
            else:
                total = sum_s[part, :]
            total += jnp.dot(onehot_s[2 + b, part, :], north_s[b], preferred_element_type=F32)
            total += jnp.dot(onehot_s[4 + b, part, :], south_s[b], preferred_element_type=F32)
            if b == 0:
                sum_s[part, :] = total
            else:
                st_s[0, part, :] = total.astype(BF16)

    for cp in loads[7:]:
        cp.wait()

    has_top = jnp.where(lat > 0, 1.0, 0.0).astype(F32)
    has_bot = jnp.where(lat < nlat - 1, 1.0, 0.0).astype(F32)

    for l in range(LAYERS):
        st = st_s.at[l]
        edge_l[l] = jnp.dot(pick_ls[...], st[...], preferred_element_type=F32).astype(BF16)
        edge_r[l] = jnp.dot(pick_rs[...], st[...], preferred_element_type=F32).astype(BF16)
        moves = [
            (st.at[pl.ds(496, 80)], top_s.at[l], (1, 0)),
            (st.at[pl.ds(0, 80)], bot_s.at[l], (-1, 0)),
            (edge_r.at[l, pl.ds(16, 80)], strip_l.at[l, pl.ds(16, 80)], (0, 1)),
            (edge_l.at[l, pl.ds(16, 80)], strip_r.at[l, pl.ds(16, 80)], (0, -1)),
            (edge_r.at[l, pl.ds(0, 16)], strip_l.at[l, pl.ds(0, 16)], (1, 1)),
            (edge_r.at[l, pl.ds(96, 16)], strip_l.at[l, pl.ds(96, 16)], (-1, 1)),
            (edge_l.at[l, pl.ds(0, 16)], strip_r.at[l, pl.ds(0, 16)], (1, -1)),
            (edge_l.at[l, pl.ds(96, 16)], strip_r.at[l, pl.ds(96, 16)], (-1, -1)),
        ]
        copies = [
            pltpu.make_async_remote_copy(src, dst, hsend.at[l, n], hrecv.at[l, n], device_id=at(*d), device_id_type=MESH)
            for n, (src, dst, d) in enumerate(moves)
        ]
        for cp in copies:
            cp.start()
        for c in range(2):
            lanes = slice(c * 128, (c + 1) * 128)
            pad_s[c, 3:27, 8:32, :] = st[:, lanes].astype(F32).reshape(T, T, 128)
        for cp in copies:
            cp.wait()
        left = jnp.dot(spread_ls[...], strip_l[l], preferred_element_type=F32).reshape(30, 8, C)
        right = jnp.dot(spread_rs[...], strip_r[l], preferred_element_type=F32).reshape(30, 8, C)
        upper = top_s[l].astype(F32)[8:80].reshape(3, T, C) * has_top
        lower = bot_s[l].astype(F32)[0:72].reshape(3, T, C) * has_bot
        for c in range(2):
            lanes = slice(c * 128, (c + 1) * 128)
            for side, lo in ((left, 0), (right, 32)):
                pad_s[c, 0:3, lo:lo + 8, :] = side[0:3, :, lanes] * has_top
                pad_s[c, 3:27, lo:lo + 8, :] = side[3:27, :, lanes]
                pad_s[c, 27:30, lo:lo + 8, :] = side[27:30, :, lanes] * has_bot
            pad_s[c, 0:3, 8:32, :] = upper[:, :, lanes]
            pad_s[c, 27:30, 8:32, :] = lower[:, :, lanes]

        def mix_rows(h0, c, l=l):
            lanes = slice(c * 128, (c + 1) * 128)
            acc = [None] * 8
            for e in range(KS):
                wt = [dep_s[a, e, l:l + 1, lanes] for a in range(KS)]
                for r in range(14):
                    line = pad_s[c, h0 + r, 5 + e:29 + e, :]
                    for a in range(KS):
                        o = r - a
                        if 0 <= o < 8:
                            term = line * wt[a]
                            acc[o] = term if acc[o] is None else acc[o] + term
            for o in range(8):
                mix_s[c, h0 + o] = acc[o]

        for c in range(2):
            def mix_step(g, _, c=c):
                mix_rows(g * 8, c)
                return 0

            lax.fori_loop(0, 3, mix_step, 0)

        for g in range(2):
            part = slice(g * 288, (g + 1) * 288)
            m0 = mix_s[0, g * 12:(g + 1) * 12].reshape(288, 128)
            m1 = mix_s[1, g * 12:(g + 1) * 12].reshape(288, 128)
            mean = jnp.sum(m0 + m1, axis=-1, keepdims=True) * (1.0 / C)
            c0, c1 = m0 - mean, m1 - mean
            var = jnp.sum(c0 * c0 + c1 * c1, axis=-1, keepdims=True) * (1.0 / C)
            inv = lax.rsqrt(var + 1e-6)
            normed = jnp.concatenate(
                [(c0 * inv * gain_s[l:l + 1, 0:128]).astype(BF16), (c1 * inv * gain_s[l:l + 1, 128:256]).astype(BF16)], axis=1
            )
            new = st[part, :].astype(F32)
            for q in range(4):
                hq = slice(q * 256, (q + 1) * 256)
                hid = gelu(jnp.dot(normed, up_s[l, :, hq], preferred_element_type=F32)).astype(BF16)
                new += jnp.dot(hid, dn_s[l, hq, :], preferred_element_type=F32)
            if l == LAYERS - 1:
                out[part, :] = new.astype(BF16)
            else:
                st_s[l + 1, part, :] = new.astype(BF16)


def solution(mesh):
    nlat, nlon = mesh.shape["lat"], mesh.shape["lon"]

    def per_device(swath, wconv, bias, band, roff, coff, roww, colw, back, depth, gain, up, down):
        smem = pl.BlockSpec(memory_space=pltpu.SMEM)
        vmem = pl.BlockSpec(memory_space=pltpu.VMEM)
        hbm = pl.BlockSpec(memory_space=pl.ANY)
        dma = pltpu.SemaphoreType.DMA
        result = pl.pallas_call(
            functools.partial(body, nlat, nlon),
            out_shape=pltpu.VMEM((CELLS, C), BF16),
            in_specs=[smem] * 3 + [hbm] * 14,
            out_specs=vmem,
            scratch_shapes=[
                pltpu.VMEM((NB, IB, IB, C), BF16),
                pltpu.VMEM((3, 3 * C, C), BF16),
                pltpu.VMEM((LAYERS, C, HID), BF16),
                pltpu.VMEM((LAYERS, HID, C), BF16),
                pltpu.VMEM((SLOTS, 2, 8, 72, 128), F32),
                pltpu.VMEM((33, 2, OB, 3 * C), BF16),
                pltpu.VMEM((OB * OB, C), BF16),
                pltpu.VMEM((NB, RB * RB, OB * OB), BF16),
                pltpu.VMEM((NB, RB * RB, C), BF16),
                pltpu.VMEM((NB, RB * RB, C), BF16),
                pltpu.VMEM((NB, RB * RB, C), BF16),
                pltpu.VMEM((3, 8, C), jnp.int32),
                pltpu.VMEM((8, C), jnp.int32),
                pltpu.VMEM((8, C), jnp.int32),
                pltpu.VMEM((3 * NB, CELLS, RB * RB), BF16),
                pltpu.VMEM((CELLS, C), jnp.int32),
                pltpu.VMEM((CELLS, C), F32),
                pltpu.VMEM((LAYERS, CELLS, C), BF16),
                pltpu.VMEM((2, 30, 40, 128), F32),
                pltpu.VMEM((2, T, T, 128), F32),
                pltpu.VMEM((LAYERS, STRIP, C), BF16),
                pltpu.VMEM((LAYERS, STRIP, C), BF16),
                pltpu.VMEM((LAYERS, STRIP, C), BF16),
                pltpu.VMEM((LAYERS, STRIP, C), BF16),
                pltpu.VMEM((LAYERS, 80, C), BF16),
                pltpu.VMEM((LAYERS, 80, C), BF16),
                pltpu.VMEM((NB, RB, OB), BF16),
                pltpu.VMEM((NB, RB, OB), BF16),
                pltpu.VMEM((1, C), F32),
                pltpu.VMEM((CELLS, C), BF16),
                pltpu.VMEM((STRIP, CELLS), BF16),
                pltpu.VMEM((STRIP, CELLS), BF16),
                pltpu.VMEM((240, STRIP), BF16),
                pltpu.VMEM((240, STRIP), BF16),
                pltpu.VMEM((KS, KS, LAYERS, C), F32),
                pltpu.VMEM((LAYERS, C), F32),
                dma((15,)),
                dma((NB, 2)),
                dma((NB, 2)),
                dma((2,)),
                dma((2,)),
                dma((LAYERS, 8)),
                dma((LAYERS, 8)),
            ],
            compiler_params=pltpu.CompilerParams(
                collective_id=0, has_side_effects=True, vmem_limit_bytes=56 * 1024 * 1024
            ),
        )(
            band.reshape(NB), roff, coff, swath, wconv.reshape(3, 3 * C, C), bias.reshape(1, C), roww, colw,
            back.reshape(CELLS, C), jnp.transpose(depth, (1, 2, 0, 3)), gain, up, down,
            jnp.asarray(pick_matrix(0), BF16), jnp.asarray(pick_matrix(T - HALO), BF16),
            jnp.asarray(spread_matrix(5), BF16), jnp.asarray(spread_matrix(0), BF16),
        )
        return result.reshape(T, T, C)

    split = P(("lat", "lon"))
    in_specs = (split, P(), P(), split, split, split, split, split, P("lat", "lon"), P(), P(), P(), P())
    return jax.shard_map(
        per_device, mesh=mesh, in_specs=in_specs, out_specs=P("lat", "lon", None), check_vma=False
    )
```

time: 63.7 us -> 58 us (0.911)
  local copies, waits for them, and re-layouts: 4.69 us -> 0.72 us
  Pallas kernels: 58.7 us -> 57.1 us
    unnamed x2 -> x1, local copies, waits for them, and re-layouts: 3.01 us -> 0.72 us
    reshape x2 -> x0, local copies, waits for them, and re-layouts: 1.69 us -> none  [per_device(): depth.reshape(LAYERS, KS, KS, 2, 128)]
    pallas_call x1, Pallas kernels: 58.7 us -> 57.1 us  [per_device(): pl.pallas_call(functools.partial(body, nlat, nlon), out_shape=pltpu.VMEM(...]
where the time goes in v2:
time: 58 us; the launch traced here: 57.8 us
  Pallas kernels  57.1 us (98%)
  local copies, waits for them, and re-layouts  0.72 us (1%)
    pallas_call x1, Pallas kernels, per_device(): pl.pallas_call(functools.partial(body, nlat, nlon), out_shape=pltpu.VMEM(...  57.1 us

profile of v2, /device:TPU:1, one launch (start us, length us, event | category | flops | bytes accessed | tf_op | source)
XLA Modules:
  0.0 57.8 jit_solution(293533883932112044)
XLA Ops:
  0.0 57.1 %shard_map.163 = bf16[576,256]{1,0:T(8,128)(2,1)S(1)} custom-call(s32[2]{0:T(128)} %bitcast.11, s32[2]{0:T(128)} %roff.1, s32[2]{0:T(128)} %coff.1, bf16[2,64,64,256]{3,2,1,0:T(8,128)(2,1)} %swath.1, bf16[3,768,256]{2,1,0:T(8,128)(2,1)} %bitcast.7, f32[1,256]{1,0:T(1,128)} %bitcast.10, bf16[2,16,32]{2,1,0:T(8,128)(2,1)} %roww.1, bf16[2,16,32]{2,1,0:T(8,128)(2,1)} %colw.1, ...), custom_call_target="tpu_custom_call" | custom-call | tf_op jit(solution)/shard_map/pallas_call | solution.py:307
  57.1 0.7 %copy.19 = bf16[24,24,256]{2,1,0:T(8,128)(2,1)} copy(bf16[24,24,256]{2,1,0:T(8,128)(2,1)S(1)} %bitcast.6) | data formatting | bytes 589824

commit v3 on v2

--- a/solution.py
+++ b/solution.py
@@ -64,7 +64,7 @@
     x_s, w_s, up_s, dn_s, t_s, x3_s, feat_s, kron_s, own_s, north_s, south_s,
     meta_s, meta_n, meta_d, onehot_s, acc_s, sum_s, st_s, pad_s, mix_s,
     edge_l, edge_r, strip_l, strip_r, top_s, bot_s,
-    roww_s, colw_s, bias_s, back_s, pick_ls, pick_rs, spread_ls, spread_rs, dep_s, gain_s,
+    roww_s, colw_s, bias_s, back_s, pick_ls, pick_rs, spread_ls, spread_rs, dep_s, gain_s, raw_s, west_s, east_s, rows_s,
     load_sem, bsend, brecv, msend, mrecv, hsend, hrecv,
 ):
     lat, lon = lax.axis_index("lat"), lax.axis_index("lon")
@@ -81,7 +81,7 @@
         for n, (src, dst) in enumerate((
             (roww, roww_s), (colw, colw_s), (swath.at[0], x_s.at[0]), (bias, bias_s), (wconv, w_s), (swath.at[1], x_s.at[1]),
             (back, back_s), (pick_l, pick_ls), (pick_r, pick_rs), (spread_l, spread_ls), (spread_r, spread_rs),
-            (depth, dep_s), (gain, gain_s), (up, up_s), (down, dn_s),
+            (depth, raw_s), (gain, gain_s), (up, up_s), (down, dn_s),
         ))
     ]
     for cp in loads:
@@ -185,6 +185,15 @@
         sends.append(pair)
 
     loads[6].wait()
+    for cp in loads[7:]:
+        cp.wait()
+    for ref in (pad_s, west_s, east_s, rows_s):
+        ref[...] = jnp.zeros(ref.shape, F32)
+    for l in range(LAYERS):
+        for c in range(2):
+            for e in range(KS):
+                for a in range(KS):
+                    dep_s[2 * l + c, a * KS + e] = jnp.broadcast_to(raw_s[a, e, l:l + 1, c * 128:(c + 1) * 128], (8, 128))
     for cp in metas:
         cp.wait()
     build_onehot(1, meta_n)
@@ -207,9 +216,6 @@
                 sum_s[part, :] = total
             else:
                 st_s[0, part, :] = total.astype(BF16)
-
-    for cp in loads[7:]:
-        cp.wait()
 
     has_top = jnp.where(lat > 0, 1.0, 0.0).astype(F32)
     has_bot = jnp.where(lat < nlat - 1, 1.0, 0.0).astype(F32)
@@ -235,44 +241,82 @@
         for cp in copies:
             cp.start()
         for c in range(2):
-            lanes = slice(c * 128, (c + 1) * 128)
-            pad_s[c, 3:27, 8:32, :] = st[:, lanes].astype(F32).reshape(T, T, 128)
-        for cp in copies:
-            cp.wait()
-        left = jnp.dot(spread_ls[...], strip_l[l], preferred_element_type=F32).reshape(30, 8, C)
-        right = jnp.dot(spread_rs[...], strip_r[l], preferred_element_type=F32).reshape(30, 8, C)
-        upper = top_s[l].astype(F32)[8:80].reshape(3, T, C) * has_top
-        lower = bot_s[l].astype(F32)[0:72].reshape(3, T, C) * has_bot
-        for c in range(2):
-            lanes = slice(c * 128, (c + 1) * 128)
-            for side, lo in ((left, 0), (right, 32)):
-                pad_s[c, 0:3, lo:lo + 8, :] = side[0:3, :, lanes] * has_top
-                pad_s[c, 3:27, lo:lo + 8, :] = side[3:27, :, lanes]
-                pad_s[c, 27:30, lo:lo + 8, :] = side[27:30, :, lanes] * has_bot
-            pad_s[c, 0:3, 8:32, :] = upper[:, :, lanes]
-            pad_s[c, 27:30, 8:32, :] = lower[:, :, lanes]
-
-        def mix_rows(h0, c, l=l):
-            lanes = slice(c * 128, (c + 1) * 128)
+            pad_s[c, 3:27, 8:32, :] = st[:, c * 128:(c + 1) * 128].astype(F32).reshape(T, T, 128)
+
+        def weights(c, e, l=l):
+            return [dep_s[2 * l + c, a * KS + e] for a in range(KS)]
+
+        def mix_own(g, _):
+            c, h0 = g // 3, (g % 3) * 8
             acc = [None] * 8
             for e in range(KS):
-                wt = [dep_s[a, e, l:l + 1, lanes] for a in range(KS)]
+                wt = weights(c, e)
                 for r in range(14):
-                    line = pad_s[c, h0 + r, 5 + e:29 + e, :]
+                    line = pad_s[c, h0 + r, 5 + e:29 + e, :].reshape(3, 8, 128)
                     for a in range(KS):
                         o = r - a
                         if 0 <= o < 8:
                             term = line * wt[a]
                             acc[o] = term if acc[o] is None else acc[o] + term
             for o in range(8):
-                mix_s[c, h0 + o] = acc[o]
-
+                mix_s[c, h0 + o] = acc[o].reshape(T, 128)
+            return 0
+
+        lax.fori_loop(0, 6, mix_own, 0)
+
+        for cp in copies[2:]:
+            cp.wait()
+        for ref, place, strip in ((west_s, spread_ls, strip_l), (east_s, spread_rs, strip_r)):
+            side = jnp.dot(place[...], strip[l], preferred_element_type=F32).reshape(30, 8, C)
+            lo = 0 if ref is west_s else 8
+            for c in range(2):
+                lanes = slice(c * 128, (c + 1) * 128)
+                ref[c, 0:3, lo:lo + 8, :] = side[0:3, :, lanes] * has_top
+                ref[c, 3:27, lo:lo + 8, :] = side[3:27, :, lanes]
+                ref[c, 27:30, lo:lo + 8, :] = side[27:30, :, lanes] * has_bot
+
+        def mix_sides(g, _):
+            c, h0 = g // 3, (g % 3) * 8
+            for ref, shifts, first, col in ((west_s, (0, 1, 2), 5, 0), (east_s, (4, 5, 6), -3, 16)):
+                acc = [mix_s[c, h0 + o, col:col + 8, :] for o in range(8)]
+                for e in shifts:
+                    wt = weights(c, e)
+                    for r in range(14):
+                        line = ref[c, h0 + r, first + e:first + e + 8, :]
+                        for a in range(KS):
+                            if 0 <= r - a < 8:
+                                acc[r - a] += line * wt[a]
+                for o in range(8):
+                    mix_s[c, h0 + o, col:col + 8, :] = acc[o]
+            return 0
+
+        lax.fori_loop(0, 6, mix_sides, 0)
+
+        for cp in copies[:2]:
+            cp.wait()
+        upper = top_s[l].astype(F32)[8:80].reshape(3, T, C) * has_top
+        lower = bot_s[l].astype(F32)[0:72].reshape(3, T, C) * has_bot
         for c in range(2):
-            def mix_step(g, _, c=c):
-                mix_rows(g * 8, c)
-                return 0
-
-            lax.fori_loop(0, 3, mix_step, 0)
+            lanes = slice(c * 128, (c + 1) * 128)
+            rows_s[0, c, :, 8:32, :] = upper[:, :, lanes]
+            rows_s[1, c, :, 8:32, :] = lower[:, :, lanes]
+
+        def mix_ends(c, _):
+            for side, h0 in ((0, 0), (1, T - HALO)):
+                acc = [mix_s[c, h0 + o].reshape(3, 8, 128) for o in range(3)]
+                for e in range(KS):
+                    wt = weights(c, e)
+                    for r in range(3):
+                        line = rows_s[side, c, r, 5 + e:29 + e, :].reshape(3, 8, 128)
+                        for o in range(3):
+                            a = r - o if side == 0 else 6 + r - o
+                            if 0 <= a < KS:
+                                acc[o] += line * wt[a]
+                for o in range(3):
+                    mix_s[c, h0 + o] = acc[o].reshape(T, 128)
+            return 0
+
+        lax.fori_loop(0, 2, mix_ends, 0)
 
         for g in range(2):
             part = slice(g * 288, (g + 1) * 288)
@@ -344,8 +388,12 @@
                 pltpu.VMEM((STRIP, CELLS), BF16),
                 pltpu.VMEM((240, STRIP), BF16),
                 pltpu.VMEM((240, STRIP), BF16),
+                pltpu.VMEM((2 * LAYERS, KS * KS, 8, 128), F32),
+                pltpu.VMEM((LAYERS, C), F32),
                 pltpu.VMEM((KS, KS, LAYERS, C), F32),
-                pltpu.VMEM((LAYERS, C), F32),
+                pltpu.VMEM((2, 30, 16, 128), F32),
+                pltpu.VMEM((2, 30, 16, 128), F32),
+                pltpu.VMEM((2, 2, 3, 40, 128), F32),
                 dma((15,)),
                 dma((NB, 2)),
                 dma((NB, 2)),

time: 58 us -> 53.9 us (0.929)
  Pallas kernels: 57.1 us -> 52.9 us
    pallas_call x1, Pallas kernels: 57.1 us -> 52.9 us  [per_device(): pl.pallas_call(functools.partial(body, nlat, nlon), out_shape=pltpu.VMEM(...]
where the time goes in v3:
time: 53.9 us; the launch traced here: 53.7 us
  Pallas kernels  52.9 us (98%)
  local copies, waits for them, and re-layouts  0.72 us (1%)
    pallas_call x1, Pallas kernels, per_device(): pl.pallas_call(functools.partial(body, nlat, nlon), out_shape=pltpu.VMEM(...  52.9 us

profile of v3, /device:TPU:1, one launch (start us, length us, event | category | flops | bytes accessed | tf_op | source)
XLA Modules:
  0.0 53.7 jit_solution(3984082349868666229)
XLA Ops:
  0.0 52.9 %shard_map.163 = bf16[576,256]{1,0:T(8,128)(2,1)S(1)} custom-call(s32[2]{0:T(128)} %bitcast.11, s32[2]{0:T(128)} %roff.1, s32[2]{0:T(128)} %coff.1, bf16[2,64,64,256]{3,2,1,0:T(8,128)(2,1)} %swath.1, bf16[3,768,256]{2,1,0:T(8,128)(2,1)} %bitcast.7, f32[1,256]{1,0:T(1,128)} %bitcast.10, bf16[2,16,32]{2,1,0:T(8,128)(2,1)} %roww.1, bf16[2,16,32]{2,1,0:T(8,128)(2,1)} %colw.1, ...), custom_call_target="tpu_custom_call" | custom-call | tf_op jit(solution)/shard_map/pallas_call | solution.py:351
  53.0 0.7 %copy.19 = bf16[24,24,256]{2,1,0:T(8,128)(2,1)} copy(bf16[24,24,256]{2,1,0:T(8,128)(2,1)S(1)} %bitcast.6) | data formatting | bytes 589824

commit v4 on v3

--- a/solution.py
+++ b/solution.py
@@ -72,9 +72,59 @@
     def at(dlat, dlon):
         return (lax.rem(lat + dlat + nlat, nlat), lax.rem(lon + dlon + nlon, nlon))
 
+    def where_band(step, action):
+        if step == 0:
+            action()
+        else:
+            pl.when(lat > 0 if step < 0 else lat < nlat - 1)(action)
+
+    def start(copies):
+        for step in (0, -1, 1):
+            def begin(step=step):
+                for d, cp in copies:
+                    if d[0] == step:
+                        cp.start()
+
+            if any(d[0] == step for d, _ in copies):
+                where_band(step, begin)
+
+    def finish(copies):
+        for step in (0, -1, 1):
+            def end(step=step):
+                for d, cp in copies:
+                    if d[0] == step:
+                        cp.wait_send()
+                    if d[0] == -step:
+                        cp.wait_recv()
+
+            if any(d[0] in (step, -step) for d, _ in copies):
+                where_band(step, end)
+
     barrier = pltpu.get_barrier_semaphore()
-    for d in DIAGS:
-        pl.semaphore_signal(barrier, inc=1, device_id=at(*d), device_id_type=MESH)
+    for step in (0, -1, 1):
+        def greet(step=step):
+            for d in DIAGS:
+                if d[0] == step:
+                    pl.semaphore_signal(barrier, inc=1, device_id=at(*d), device_id_type=MESH)
+
+        where_band(step, greet)
+
+    @pl.when(lat == 0)
+    def _():
+        top_s[...] = jnp.zeros(top_s.shape, BF16)
+        north_s[...] = jnp.zeros(north_s.shape, BF16)
+        meta_n[...] = jnp.full(meta_n.shape, -4096, jnp.int32)
+        for ref in (strip_l, strip_r):
+            ref[:, 0:16, :] = jnp.zeros((LAYERS, 16, C), BF16)
+
+    @pl.when(lat == nlat - 1)
+    def _():
+        bot_s[...] = jnp.zeros(bot_s.shape, BF16)
+        south_s[...] = jnp.zeros(south_s.shape, BF16)
+        meta_d[...] = jnp.full(meta_d.shape, -4096, jnp.int32)
+        for ref in (strip_l, strip_r):
+            ref[:, 96:112, :] = jnp.zeros((LAYERS, 16, C), BF16)
+
 
     loads = [
         pltpu.make_async_copy(src, dst, load_sem.at[n])
@@ -169,19 +219,19 @@
             conv_rows(g)
         own_s[b] = jnp.dot(kron_s[b], feat_s[...], preferred_element_type=F32).astype(BF16)
         if b == 0:
-            pl.semaphore_wait(barrier, len(DIAGS))
+            at_end = (lat == 0) | (lat == nlat - 1)
+            pl.when(at_end)(lambda: pl.semaphore_wait(barrier, 5))
+            pl.when(jnp.logical_not(at_end))(lambda: pl.semaphore_wait(barrier, 8))
             metas = [
-                pltpu.make_async_remote_copy(meta_s.at[1], meta_d, msend.at[0], mrecv.at[0], device_id=at(-1, 0), device_id_type=MESH),
-                pltpu.make_async_remote_copy(meta_s.at[2], meta_n, msend.at[1], mrecv.at[1], device_id=at(1, 0), device_id_type=MESH),
+                ((-1, 0), pltpu.make_async_remote_copy(meta_s.at[1], meta_d, msend.at[0], mrecv.at[0], device_id=at(-1, 0), device_id_type=MESH)),
+                ((1, 0), pltpu.make_async_remote_copy(meta_s.at[2], meta_n, msend.at[1], mrecv.at[1], device_id=at(1, 0), device_id_type=MESH)),
             ]
-            for cp in metas:
-                cp.start()
+            start(metas)
         pair = [
-            pltpu.make_async_remote_copy(own_s.at[b], south_s.at[b], bsend.at[b, 0], brecv.at[b, 0], device_id=at(-1, 0), device_id_type=MESH),
-            pltpu.make_async_remote_copy(own_s.at[b], north_s.at[b], bsend.at[b, 1], brecv.at[b, 1], device_id=at(1, 0), device_id_type=MESH),
+            ((-1, 0), pltpu.make_async_remote_copy(own_s.at[b], south_s.at[b], bsend.at[b, 0], brecv.at[b, 0], device_id=at(-1, 0), device_id_type=MESH)),
+            ((1, 0), pltpu.make_async_remote_copy(own_s.at[b], north_s.at[b], bsend.at[b, 1], brecv.at[b, 1], device_id=at(1, 0), device_id_type=MESH)),
         ]
-        for cp in pair:
-            cp.start()
+        start(pair)
         sends.append(pair)
 
     loads[6].wait()
@@ -194,14 +244,12 @@
             for e in range(KS):
                 for a in range(KS):
                     dep_s[2 * l + c, a * KS + e] = jnp.broadcast_to(raw_s[a, e, l:l + 1, c * 128:(c + 1) * 128], (8, 128))
-    for cp in metas:
-        cp.wait()
+    finish(metas)
     build_onehot(1, meta_n)
     build_onehot(2, meta_d)
 
     for b in range(NB):
-        for cp in sends[b]:
-            cp.wait()
+        finish(sends[b])
         for q in range(3):
             part = slice(q * 192, (q + 1) * 192)
             if b == 0:
@@ -216,9 +264,6 @@
                 sum_s[part, :] = total
             else:
                 st_s[0, part, :] = total.astype(BF16)
-
-    has_top = jnp.where(lat > 0, 1.0, 0.0).astype(F32)
-    has_bot = jnp.where(lat < nlat - 1, 1.0, 0.0).astype(F32)
 
     for l in range(LAYERS):
         st = st_s.at[l]
@@ -235,11 +280,10 @@
             (edge_l.at[l, pl.ds(96, 16)], strip_r.at[l, pl.ds(96, 16)], (-1, -1)),
         ]
         copies = [
-            pltpu.make_async_remote_copy(src, dst, hsend.at[l, n], hrecv.at[l, n], device_id=at(*d), device_id_type=MESH)
+            (d, pltpu.make_async_remote_copy(src, dst, hsend.at[l, n], hrecv.at[l, n], device_id=at(*d), device_id_type=MESH))
             for n, (src, dst, d) in enumerate(moves)
         ]
-        for cp in copies:
-            cp.start()
+        start(copies)
         for c in range(2):
             pad_s[c, 3:27, 8:32, :] = st[:, c * 128:(c + 1) * 128].astype(F32).reshape(T, T, 128)
 
@@ -264,16 +308,13 @@
 
         lax.fori_loop(0, 6, mix_own, 0)
 
-        for cp in copies[2:]:
-            cp.wait()
+        finish(copies[2:])
         for ref, place, strip in ((west_s, spread_ls, strip_l), (east_s, spread_rs, strip_r)):
             side = jnp.dot(place[...], strip[l], preferred_element_type=F32).reshape(30, 8, C)
             lo = 0 if ref is west_s else 8
             for c in range(2):
                 lanes = slice(c * 128, (c + 1) * 128)
-                ref[c, 0:3, lo:lo + 8, :] = side[0:3, :, lanes] * has_top
-                ref[c, 3:27, lo:lo + 8, :] = side[3:27, :, lanes]
-                ref[c, 27:30, lo:lo + 8, :] = side[27:30, :, lanes] * has_bot
+                ref[c, :, lo:lo + 8, :] = side[:, :, lanes]
 
         def mix_sides(g, _):
             c, h0 = g // 3, (g % 3) * 8
@@ -292,10 +333,9 @@
 
         lax.fori_loop(0, 6, mix_sides, 0)
 
-        for cp in copies[:2]:
-            cp.wait()
-        upper = top_s[l].astype(F32)[8:80].reshape(3, T, C) * has_top
-        lower = bot_s[l].astype(F32)[0:72].reshape(3, T, C) * has_bot
+        finish(copies[:2])
+        upper = top_s[l].astype(F32)[8:80].reshape(3, T, C)
+        lower = bot_s[l].astype(F32)[0:72].reshape(3, T, C)
         for c in range(2):
             lanes = slice(c * 128, (c + 1) * 128)
             rows_s[0, c, :, 8:32, :] = upper[:, :, lanes]

time: 53.9 us -> 50.8 us (0.942)
  the two profiles are of different devices: /device:TPU:1 before, /device:TPU:33 now
where the time goes in v4:
time: 50.8 us; the launch traced here: 50.6 us
  Pallas kernels  49.9 us (98%)
  local copies, waits for them, and re-layouts  0.72 us (1%)
    pallas_call x1, Pallas kernels, per_device(): pl.pallas_call(functools.partial(body, nlat, nlon), out_shape=pltpu.VMEM(...  49.9 us

profile of v4, /device:TPU:33, one launch (start us, length us, event | category | flops | bytes accessed | tf_op | source)
XLA Modules:
  0.0 50.6 jit_solution(13958633465852171624)
XLA Ops:
  0.0 49.9 %shard_map.163 = bf16[576,256]{1,0:T(8,128)(2,1)S(1)} custom-call(s32[2]{0:T(128)} %bitcast.11, s32[2]{0:T(128)} %roff.1, s32[2]{0:T(128)} %coff.1, bf16[2,64,64,256]{3,2,1,0:T(8,128)(2,1)} %swath.1, bf16[3,768,256]{2,1,0:T(8,128)(2,1)} %bitcast.7, f32[1,256]{1,0:T(1,128)} %bitcast.10, bf16[2,16,32]{2,1,0:T(8,128)(2,1)} %roww.1, bf16[2,16,32]{2,1,0:T(8,128)(2,1)} %colw.1, ...), custom_call_target="tpu_custom_call" | custom-call | tf_op jit(solution)/shard_map/pallas_call | solution.py:391
  49.9 0.7 %copy.19 = bf16[24,24,256]{2,1,0:T(8,128)(2,1)} copy(bf16[24,24,256]{2,1,0:T(8,128)(2,1)S(1)} %bitcast.6) | data formatting | bytes 589824

commit v5 on v4

--- a/solution.py
+++ b/solution.py
@@ -79,7 +79,7 @@
             pl.when(lat > 0 if step < 0 else lat < nlat - 1)(action)
 
     def start(copies):
-        for step in (0, -1, 1):
+        for step in (-1, 1, 0):
             def begin(step=step):
                 for d, cp in copies:
                     if d[0] == step:
@@ -265,10 +265,8 @@
             else:
                 st_s[0, part, :] = total.astype(BF16)
 
-    for l in range(LAYERS):
+    def halo_copies(l):
         st = st_s.at[l]
-        edge_l[l] = jnp.dot(pick_ls[...], st[...], preferred_element_type=F32).astype(BF16)
-        edge_r[l] = jnp.dot(pick_rs[...], st[...], preferred_element_type=F32).astype(BF16)
         moves = [
             (st.at[pl.ds(496, 80)], top_s.at[l], (1, 0)),
             (st.at[pl.ds(0, 80)], bot_s.at[l], (-1, 0)),
@@ -279,11 +277,19 @@
             (edge_l.at[l, pl.ds(0, 16)], strip_r.at[l, pl.ds(0, 16)], (1, -1)),
             (edge_l.at[l, pl.ds(96, 16)], strip_r.at[l, pl.ds(96, 16)], (-1, -1)),
         ]
-        copies = [
+        return [
             (d, pltpu.make_async_remote_copy(src, dst, hsend.at[l, n], hrecv.at[l, n], device_id=at(*d), device_id_type=MESH))
             for n, (src, dst, d) in enumerate(moves)
         ]
-        start(copies)
+
+    halos = [halo_copies(l) for l in range(LAYERS)]
+    start(halos[0][:2])
+    for l in range(LAYERS):
+        st = st_s.at[l]
+        copies = halos[l]
+        edge_l[l] = jnp.dot(pick_ls[...], st[...], preferred_element_type=F32).astype(BF16)
+        edge_r[l] = jnp.dot(pick_rs[...], st[...], preferred_element_type=F32).astype(BF16)
+        start(copies[2:])
         for c in range(2):
             pad_s[c, 3:27, 8:32, :] = st[:, c * 128:(c + 1) * 128].astype(F32).reshape(T, T, 128)
 
@@ -291,22 +297,22 @@
             return [dep_s[2 * l + c, a * KS + e] for a in range(KS)]
 
         def mix_own(g, _):
-            c, h0 = g // 3, (g % 3) * 8
-            acc = [None] * 8
+            c, h0 = g // 6, (g % 6) * 4
+            acc = [None] * 4
             for e in range(KS):
                 wt = weights(c, e)
-                for r in range(14):
+                for r in range(10):
                     line = pad_s[c, h0 + r, 5 + e:29 + e, :].reshape(3, 8, 128)
                     for a in range(KS):
                         o = r - a
-                        if 0 <= o < 8:
+                        if 0 <= o < 4:
                             term = line * wt[a]
                             acc[o] = term if acc[o] is None else acc[o] + term
-            for o in range(8):
+            for o in range(4):
                 mix_s[c, h0 + o] = acc[o].reshape(T, 128)
             return 0
 
-        lax.fori_loop(0, 6, mix_own, 0)
+        lax.fori_loop(0, 12, mix_own, 0)
 
         finish(copies[2:])
         for ref, place, strip in ((west_s, spread_ls, strip_l), (east_s, spread_rs, strip_r)):
@@ -358,10 +364,8 @@
 
         lax.fori_loop(0, 2, mix_ends, 0)
 
-        for g in range(2):
-            part = slice(g * 288, (g + 1) * 288)
-            m0 = mix_s[0, g * 12:(g + 1) * 12].reshape(288, 128)
-            m1 = mix_s[1, g * 12:(g + 1) * 12].reshape(288, 128)
+        for spans in (((0, 4), (20, 24)), ((4, 20),)):
+            m0, m1 = (jnp.concatenate([mix_s[c, lo:hi] for lo, hi in spans], axis=0).reshape(-1, 128) for c in range(2))
             mean = jnp.sum(m0 + m1, axis=-1, keepdims=True) * (1.0 / C)
             c0, c1 = m0 - mean, m1 - mean
             var = jnp.sum(c0 * c0 + c1 * c1, axis=-1, keepdims=True) * (1.0 / C)
@@ -369,15 +373,18 @@
             normed = jnp.concatenate(
                 [(c0 * inv * gain_s[l:l + 1, 0:128]).astype(BF16), (c1 * inv * gain_s[l:l + 1, 128:256]).astype(BF16)], axis=1
             )
-            new = st[part, :].astype(F32)
+            new = jnp.concatenate([st[lo * T:hi * T, :] for lo, hi in spans], axis=0).astype(F32)
             for q in range(4):
                 hq = slice(q * 256, (q + 1) * 256)
                 hid = gelu(jnp.dot(normed, up_s[l, :, hq], preferred_element_type=F32)).astype(BF16)
                 new += jnp.dot(hid, dn_s[l, hq, :], preferred_element_type=F32)
-            if l == LAYERS - 1:
-                out[part, :] = new.astype(BF16)
-            else:
-                st_s[l + 1, part, :] = new.astype(BF16)
+            target = out if l == LAYERS - 1 else st_s.at[l + 1]
+            first = 0
+            for lo, hi in spans:
+                target[lo * T:hi * T, :] = new[first:first + (hi - lo) * T].astype(BF16)
+                first += (hi - lo) * T
+            if l < LAYERS - 1 and len(spans) == 2:
+                start(halos[l + 1][:2])
 
 
 def solution(mesh):

time: 50.8 us -> 50.3 us (level)
    pallas_call x1, Pallas kernels: 49.9 us -> 49.4 us  [per_device(): pl.pallas_call(functools.partial(body, nlat, nlon), out_shape=pltpu.VMEM(...]
where the time goes in v5:
time: 50.3 us; the launch traced here: 50.1 us
  Pallas kernels  49.4 us (98%)
  local copies, waits for them, and re-layouts  0.72 us (1%)
    pallas_call x1, Pallas kernels, per_device(): pl.pallas_call(functools.partial(body, nlat, nlon), out_shape=pltpu.VMEM(...  49.4 us

profile of v5, /device:TPU:33, one launch (start us, length us, event | category | flops | bytes accessed | tf_op | source)
XLA Modules:
  0.0 50.1 jit_solution(8415280092849379524)
XLA Ops:
  0.0 49.4 %shard_map.163 = bf16[576,256]{1,0:T(8,128)(2,1)S(1)} custom-call(s32[2]{0:T(128)} %bitcast.11, s32[2]{0:T(128)} %roff.1, s32[2]{0:T(128)} %coff.1, bf16[2,64,64,256]{3,2,1,0:T(8,128)(2,1)} %swath.1, bf16[3,768,256]{2,1,0:T(8,128)(2,1)} %bitcast.7, f32[1,256]{1,0:T(1,128)} %bitcast.10, bf16[2,16,32]{2,1,0:T(8,128)(2,1)} %roww.1, bf16[2,16,32]{2,1,0:T(8,128)(2,1)} %colw.1, ...), custom_call_target="tpu_custom_call" | custom-call | tf_op jit(solution)/shard_map/pallas_call | solution.py:398
  49.4 0.7 %copy.19 = bf16[24,24,256]{2,1,0:T(8,128)(2,1)} copy(bf16[24,24,256]{2,1,0:T(8,128)(2,1)S(1)} %bitcast.6) | data formatting | bytes 589824
